TPU v7x, 128 devices: a whole 4x4x4 slice. The times are simulated.
128 devices in a mesh: dp: 16 (over x, y), expert: 8 (over z, core).
Axes of the slice: x: 4, y: 4, z: 4, core: 2. Of those that a mesh axis runs over, the one named last changes fastest.
Arguments:
- tokens: bfloat16 [16, 2048, 768], P('dp', 'expert'), may hold values from -6 to 6
- group_kind: int32 [16], P('dp'), may hold values from 0 to 1, as said below
- routes: int32 [16, 2048, 2], P('dp', 'expert'), may hold values from 0 to 15, all different within a row
- norm1_gain: float32 [768], replicated, may hold values from 0.1 to 1.9
- qkv_weight: bfloat16 [768, 2304], replicated, may hold values from -0.21875 to 0.21875
- proj_weight: bfloat16 [768, 768], replicated, may hold values from -2.5 to 2.5
- norm2_gain: float32 [768], replicated, may hold values from 0.1 to 1.9
- router_weight: bfloat16 [768, 16], replicated, may hold values from -0.15625 to 0.15625
- frozen_in: bfloat16 [8, 768, 3072], P('expert'), may hold values from -0.21875 to 0.21875
- frozen_out: bfloat16 [8, 3072, 768], P('expert'), may hold values from -0.15625 to 0.15625
- new_in: bfloat16 [8, 768, 3072], P('expert'), may hold values from -0.21875 to 0.21875
- new_out: bfloat16 [8, 3072, 768], P('expert'), may hold values from -0.15625 to 0.15625
- out_grad: bfloat16 [16, 2048, 768], P('dp', 'expert'), may hold values from -6 to 6
Outputs:
- mixed: bfloat16 [16, 2048, 768], P('dp', 'expert')
- tokens_grad: float32 [16, 2048, 768], P('dp', 'expert')
- norm1_gain_grad: float32 [768], P(('dp', 'expert'))
- qkv_grad: float32 [768, 2304], P(('dp', 'expert'))
- proj_grad: float32 [768, 768], P(('dp', 'expert'))
- norm2_gain_grad: float32 [768], P(('dp', 'expert'))
- router_grad: float32 [768, 16], P(('dp', 'expert'))
- new_in_grad: float32 [8, 768, 3072], P('expert', 'dp')
- new_out_grad: float32 [8, 3072, 768], P('expert', 'dp')
Inputs may be any that keep to these rules, and one draw needn't show every extreme that they name: `group_kind`: exactly half of the 16 groups are of kind 1. `routes`: the two experts of a token differ.
All inputs are finite; a program needn't handle non-finite values.
Results may differ from a plain program's by a relative error of at most 0.017.
Values may be sent and summed in bfloat16 or wider, within the bound.
A program may use at most 256 MiB of HBM per device.

v0:
```python
import jax
import jax.numpy as jnp
from jax import lax
from jax.sharding import PartitionSpec as P

HEADS = 12
HD = 64
TOP = 2
LONG = 2048


epsilon = 1e-05


def norm_parts(values):
    average = jnp.mean(values, axis=-1, keepdims=True)
    centred = values - average
    variance = jnp.mean(centred * centred, axis=-1, keepdims=True)
    inverse = lax.rsqrt(variance + epsilon)
    return (centred * inverse, inverse)


def norm_back(grad_normed, normed, inverse):
    first_mean = jnp.mean(grad_normed, axis=-1, keepdims=True)
    second_mean = jnp.mean(grad_normed * normed, axis=-1, keepdims=True)
    return inverse * (grad_normed - first_mean - normed * second_mean)


def gelu_slope(pre_act):
    cumulative = 0.5 * (1.0 + lax.erf(pre_act * 0.7071067811865476))
    density = jnp.exp(-0.5 * pre_act * pre_act) * 0.3989422804014327
    return cumulative + pre_act * density


def mask_between(seq_kind, query_pos, key_pos):
    half_length = LONG // 2
    query_seq = seq_kind * (query_pos // half_length)
    key_seq = seq_kind * (key_pos // half_length)
    return (key_pos[None, :] <= query_pos[:, None]) & (key_seq[None, :] == query_seq[:, None])


def masked_scores(queries, keys, seq_kind, query_start, score_scale):
    query_rows = queries.shape[0]
    key_rows = keys.shape[0]
    query_heads = queries.reshape(query_rows, HEADS, HD)
    key_heads = keys.reshape(key_rows, HEADS, HD)
    scores = (
        jnp.einsum("qhd,khd->hqk", query_heads, key_heads, preferred_element_type=jnp.float32)
        * score_scale
    )
    query_pos = query_start + jnp.arange(query_rows, dtype=jnp.int32)
    key_pos = jnp.arange(key_rows, dtype=jnp.int32)
    allowed = mask_between(seq_kind, query_pos, key_pos)
    return jnp.where(allowed[None], scores, -1e30)


def attend_group(queries, keys_whole, values_whole, seq_kind, start_row, score_scale):
    rows_here = queries.shape[0]
    length = keys_whole.shape[0]
    masked = masked_scores(queries, keys_whole, seq_kind, start_row, score_scale)
    row_max = jnp.max(masked, axis=-1, keepdims=True)
    exponent = jnp.exp(masked - row_max)
    row_total = jnp.sum(exponent, axis=-1, keepdims=True)
    probs = (exponent / row_total).astype(jnp.bfloat16)
    value_heads = values_whole.reshape(length, HEADS, HD)
    attended = jnp.einsum("hqk,khd->qhd", probs, value_heads, preferred_element_type=jnp.float32)
    return (
        attended.reshape(rows_here, HEADS * HD).astype(jnp.bfloat16),
        row_max + jnp.log(row_total),
    )


def query_part(
    queries, keys_whole, values_whole, seq_kind, start_row, score_scale, log_totals, grad_att
):
    rows_here = queries.shape[0]
    length = keys_whole.shape[0]
    masked = masked_scores(queries, keys_whole, seq_kind, start_row, score_scale)
    probs = jnp.exp(masked - log_totals)
    key_heads = keys_whole.reshape(length, HEADS, HD)
    value_heads = values_whole.reshape(length, HEADS, HD)
    grad_heads = grad_att.reshape(rows_here, HEADS, HD)
    grad_probs = jnp.einsum(
        "qhd,khd->hqk", grad_heads, value_heads, preferred_element_type=jnp.float32
    )
    row_delta = jnp.sum(probs * grad_probs, axis=-1, keepdims=True)
    grad_scores = (probs * (grad_probs - row_delta)).astype(jnp.bfloat16)
    grad_query = (
        jnp.einsum("hqk,khd->qhd", grad_scores, key_heads, preferred_element_type=jnp.float32)
        * score_scale
    )
    return (grad_query.reshape(rows_here, HEADS * HD), row_delta, probs, grad_scores)


def attend_back(
    queries, keys_whole, values_whole, seq_kind, start_row, score_scale, log_totals, grad_att
):
    rows_here = queries.shape[0]
    grad_query, row_delta, probs, grad_scores = query_part(
        queries, keys_whole, values_whole, seq_kind, start_row, score_scale, log_totals, grad_att
    )
    length = keys_whole.shape[0]
    query_heads = queries.reshape(rows_here, HEADS, HD)
    grad_heads = grad_att.reshape(rows_here, HEADS, HD)
    grad_key = (
        jnp.einsum("hqk,qhd->khd", grad_scores, query_heads, preferred_element_type=jnp.float32)
        * score_scale
    )
    grad_value = jnp.einsum(
        "hqk,qhd->khd", probs.astype(jnp.bfloat16), grad_heads, preferred_element_type=jnp.float32
    )
    return (
        grad_query,
        grad_key.reshape(length, HEADS * HD),
        grad_value.reshape(length, HEADS * HD),
    )


def routing(routes, capacity, experts):
    expert_ids = jnp.arange(experts, dtype=jnp.int32)
    pick_zero = (routes[..., 0:1] == expert_ids).astype(jnp.int32)
    pick_one = (routes[..., 1:2] == expert_ids).astype(jnp.int32)
    named_count = pick_zero + pick_one
    earlier = jnp.cumsum(named_count, axis=1) - named_count
    slot_zero = jnp.sum(earlier * pick_zero, axis=-1)
    slot_one = jnp.sum(earlier * pick_one, axis=-1)
    columns = jnp.arange(experts * capacity, dtype=jnp.int32)
    target_zero = routes[..., 0] * capacity + slot_zero
    target_one = routes[..., 1] * capacity + slot_one
    send_zero = ((target_zero[..., None] == columns) & (slot_zero < capacity)[..., None]).astype(
        jnp.float32
    )
    send_one = ((target_one[..., None] == columns) & (slot_one < capacity)[..., None]).astype(
        jnp.float32
    )
    return (pick_zero.astype(jnp.float32), pick_one.astype(jnp.float32), send_zero, send_one)


def sum_experts(in_grad, out_grad_weights):
    return (
        lax.psum_scatter(
            in_grad[None].astype(jnp.bfloat16), "dp", scatter_dimension=1, tiled=True
        ).astype(jnp.float32),
        lax.psum_scatter(
            out_grad_weights[None].astype(jnp.bfloat16), "dp", scatter_dimension=1, tiled=True
        ).astype(jnp.float32),
    )


def on_device(
    tokens,
    group_kind,
    routes,
    norm1_gain,
    qkv_weight,
    proj_weight,
    norm2_gain,
    router_weight,
    frozen_in,
    frozen_out,
    new_in,
    new_out,
    out_grad,
):
    groups, rows, width = tokens.shape
    count = lax.axis_size("expert")
    experts = 2 * count
    capacity = max(2, 3 * rows * TOP // (2 * experts))
    start_row = lax.axis_index("expert") * rows
    score_scale = HD ** (-0.5)
    inputs = tokens.astype(jnp.float32)
    normed_one, inverse_one = norm_parts(inputs)
    hidden_one = (normed_one * norm1_gain).astype(jnp.bfloat16)
    projected = jnp.einsum(
        "gtd,de->gte", hidden_one, qkv_weight, preferred_element_type=jnp.float32
    ).astype(jnp.bfloat16)
    queries = projected[..., :width]
    keys_local = projected[..., width : 2 * width]
    values_local = projected[..., 2 * width :]
    keys_whole, values_whole = (
        lax.all_gather(keys_local, "expert", axis=1, tiled=True),
        lax.all_gather(values_local, "expert", axis=1, tiled=True),
    )

    def forward_group(group_items):
        query_rows, key_rows, value_rows, seq_kind = group_items
        return attend_group(query_rows, key_rows, value_rows, seq_kind, start_row, score_scale)

    attended, log_totals = lax.map(forward_group, (queries, keys_whole, values_whole, group_kind))
    branch = jnp.einsum("gtd,de->gte", attended, proj_weight, preferred_element_type=jnp.float32)
    residual = inputs + branch
    normed_two, inverse_two = norm_parts(residual)
    hidden_two = (normed_two * norm2_gain).astype(jnp.bfloat16)
    logits = jnp.einsum(
        "gtd,de->gte", hidden_two, router_weight, preferred_element_type=jnp.float32
    )
    pick_zero, pick_one, send_zero, send_one = routing(routes, capacity, experts)
    logit_zero = jnp.sum(logits * pick_zero, axis=-1)
    logit_one = jnp.sum(logits * pick_one, axis=-1)
    gate_zero = jax.nn.sigmoid(logit_zero - logit_one)
    gate_one = jax.nn.sigmoid(logit_one - logit_zero)
    dispatch = (send_zero + send_one).astype(jnp.bfloat16)
    buffers = jnp.einsum(
        "gts,gtd->gsd", dispatch, hidden_two, preferred_element_type=jnp.float32
    ).astype(jnp.bfloat16)
    buffers = buffers.reshape(groups, 2, count, capacity, width)
    received = lax.all_to_all(buffers, "expert", split_axis=2, concat_axis=2, tiled=True)
    pre_frozen = jnp.einsum(
        "gnsd,df->gnsf", received[:, 0], frozen_in[0], preferred_element_type=jnp.float32
    )
    pre_new = jnp.einsum(
        "gnsd,df->gnsf", received[:, 1], new_in[0], preferred_element_type=jnp.float32
    )
    act_frozen = jax.nn.gelu(pre_frozen, approximate=False).astype(jnp.bfloat16)
    act_new = jax.nn.gelu(pre_new, approximate=False).astype(jnp.bfloat16)
    out_frozen = jnp.einsum(
        "gnsf,fd->gnsd", act_frozen, frozen_out[0], preferred_element_type=jnp.float32
    )
    out_new = jnp.einsum("gnsf,fd->gnsd", act_new, new_out[0], preferred_element_type=jnp.float32)
    results = jnp.stack([out_frozen, out_new], axis=1).astype(jnp.bfloat16)
    coming_back = lax.all_to_all(results, "expert", split_axis=2, concat_axis=2, tiled=True)
    returned, received, pre_act, activated = (
        coming_back,
        received,
        jnp.stack([pre_frozen, pre_new], axis=1),
        jnp.stack([act_frozen, act_new], axis=1),
    )
    returned_flat = returned.reshape(groups, experts * capacity, width)
    mixing = (gate_zero[..., None] * send_zero + gate_one[..., None] * send_one).astype(
        jnp.bfloat16
    )
    combined = jnp.einsum("gts,gsd->gtd", mixing, returned_flat, preferred_element_type=jnp.float32)
    mixed = (residual + combined).astype(jnp.bfloat16)
    grad_res = out_grad.astype(jnp.float32)
    grad_mixing = jnp.einsum(
        "gtd,gsd->gts", out_grad, returned_flat, preferred_element_type=jnp.float32
    )
    grad_returned = jnp.einsum(
        "gts,gtd->gsd", mixing, out_grad, preferred_element_type=jnp.float32
    ).astype(jnp.bfloat16)
    grad_returned = grad_returned.reshape(groups, 2, count, capacity, width)
    grad_gap = (
        (jnp.sum(grad_mixing * send_zero, axis=-1) - jnp.sum(grad_mixing * send_one, axis=-1))
        * gate_zero
        * gate_one
    )
    grad_logits = (grad_gap[..., None] * (pick_zero - pick_one)).astype(jnp.bfloat16)
    router_grad = jnp.einsum(
        "gtd,gte->de", hidden_two, grad_logits, preferred_element_type=jnp.float32
    )
    grad_hidden_two = jnp.einsum(
        "gte,de->gtd", grad_logits, router_weight, preferred_element_type=jnp.float32
    )
    arriving = lax.all_to_all(grad_returned, "expert", split_axis=2, concat_axis=2, tiled=True)
    grad_act_frozen = jnp.einsum(
        "gnsd,fd->gnsf", arriving[:, 0], frozen_out[0], preferred_element_type=jnp.float32
    )
    grad_act_new = jnp.einsum(
        "gnsd,fd->gnsf", arriving[:, 1], new_out[0], preferred_element_type=jnp.float32
    )
    grad_pre_frozen = (grad_act_frozen * gelu_slope(pre_act[:, 0])).astype(jnp.bfloat16)
    grad_pre_new = (grad_act_new * gelu_slope(pre_act[:, 1])).astype(jnp.bfloat16)
    new_out_grad = jnp.einsum(
        "gnsf,gnsd->fd", activated[:, 1], arriving[:, 1], preferred_element_type=jnp.float32
    )
    new_in_grad = jnp.einsum(
        "gnsd,gnsf->df", received[:, 1], grad_pre_new, preferred_element_type=jnp.float32
    )
    grad_in_frozen = jnp.einsum(
        "gnsf,df->gnsd", grad_pre_frozen, frozen_in[0], preferred_element_type=jnp.float32
    )
    grad_in_new = jnp.einsum(
        "gnsf,df->gnsd", grad_pre_new, new_in[0], preferred_element_type=jnp.float32
    )
    grad_received = jnp.stack([grad_in_frozen, grad_in_new], axis=1).astype(jnp.bfloat16)
    sent_back = lax.all_to_all(grad_received, "expert", split_axis=2, concat_axis=2, tiled=True)
    grad_hidden_two = grad_hidden_two + jnp.einsum(
        "gts,gsd->gtd",
        dispatch,
        sent_back.reshape(groups, experts * capacity, width),
        preferred_element_type=jnp.float32,
    )
    norm2_gain_grad = jnp.sum(grad_hidden_two * normed_two, axis=(0, 1))
    grad_residual = grad_res + norm_back(grad_hidden_two * norm2_gain, normed_two, inverse_two)
    grad_branch = grad_residual.astype(jnp.bfloat16)
    proj_grad = jnp.einsum("gtd,gte->de", attended, grad_branch, preferred_element_type=jnp.float32)
    grad_attended = jnp.einsum(
        "gte,de->gtd", grad_branch, proj_weight, preferred_element_type=jnp.float32
    ).astype(jnp.bfloat16)
    keys_back, values_back = (keys_whole, values_whole)

    def backward_group(group_items):
        query_rows, key_rows, value_rows, seq_kind, group_totals, grad_rows = group_items
        return attend_back(
            query_rows,
            key_rows,
            value_rows,
            seq_kind,
            start_row,
            score_scale,
            group_totals,
            grad_rows,
        )

    grad_queries, grad_keys_whole, grad_values_whole = lax.map(
        backward_group, (queries, keys_back, values_back, group_kind, log_totals, grad_attended)
    )
    grad_keys, grad_values = (
        lax.psum_scatter(
            grad_keys_whole.astype(jnp.bfloat16), "expert", scatter_dimension=1, tiled=True
        ).astype(jnp.float32),
        lax.psum_scatter(
            grad_values_whole.astype(jnp.bfloat16), "expert", scatter_dimension=1, tiled=True
        ).astype(jnp.float32),
    )
    grad_projected = jnp.concatenate(
        [
            grad_queries.astype(jnp.bfloat16),
            grad_keys.astype(jnp.bfloat16),
            grad_values.astype(jnp.bfloat16),
        ],
        axis=-1,
    )
    qkv_grad = jnp.einsum(
        "gtd,gte->de", hidden_one, grad_projected, preferred_element_type=jnp.float32
    )
    grad_hidden_one = jnp.einsum(
        "gte,de->gtd", grad_projected, qkv_weight, preferred_element_type=jnp.float32
    )
    norm1_gain_grad = jnp.sum(grad_hidden_one * normed_one, axis=(0, 1))
    tokens_grad = grad_residual + norm_back(grad_hidden_one * norm1_gain, normed_one, inverse_one)
    expert_sums = sum_experts(new_in_grad, new_out_grad)
    dense_sums = (
        lax.psum_scatter(norm1_gain_grad, ("dp", "expert"), scatter_dimension=0, tiled=True),
        lax.psum_scatter(qkv_grad, ("dp", "expert"), scatter_dimension=0, tiled=True),
        lax.psum_scatter(proj_grad, ("dp", "expert"), scatter_dimension=0, tiled=True),
        lax.psum_scatter(norm2_gain_grad, ("dp", "expert"), scatter_dimension=0, tiled=True),
        lax.psum_scatter(router_grad, ("dp", "expert"), scatter_dimension=0, tiled=True),
    )
    return (
        mixed,
        tokens_grad,
        dense_sums[0],
        dense_sums[1],
        dense_sums[2],
        dense_sums[3],
        dense_sums[4],
        expert_sums[0],
        expert_sums[1],
    )


def solution(mesh):
    return jax.shard_map(
        on_device,
        mesh=mesh,
        in_specs=(
            P("dp", "expert", None),
            P("dp"),
            P("dp", "expert", None),
            P(),
            P(),
            P(),
            P(),
            P(),
            P("expert", None, None),
            P("expert", None, None),
            P("expert", None, None),
            P("expert", None, None),
            P("dp", "expert", None),
        ),
        out_specs=(
            P("dp", "expert", None),
            P("dp", "expert", None),
            P(("dp", "expert")),
            P(("dp", "expert"), None),
            P(("dp", "expert"), None),
            P(("dp", "expert")),
            P(("dp", "expert"), None),
            P("expert", "dp", None),
            P("expert", "dp", None),
        ),
        check_vma=False,
    )
```

profile of v0, /device:TPU:0, one launch (start us, length us, event | category | flops | bytes accessed | tf_op | source)
XLA Modules:
  0.0 1091.6 jit_solution(13780346428085370506)
XLA Ops:
  25.1 18.5 %all-gather.5.cloned.1.call-done = bf16[1,2048,768]{2,1,0:T(8,128)(2,1)} async-done(((bf16[1,256,768]{2,1,0:T(8,128)(2,1)}), bf16[1,2048,768]{2,1,0:T(8,128)(2,1)}) %all-gather.5.cloned.1.call-update) | async-done | bytes 3145744 | tf_op jit(solution)/shard_map/all_gather | solution.py:181
  43.6 4.8 copy.54
  48.4 15.3 %fusion.8 = (f32[12,256]{1,0:T(8,128)S(1)}, f32[12,256,2048]{2,1,0:T(8,128)}) fusion(pred[256,2048]{1,0:T(8,128)(4,1)} %fusion.97, bf16[256,12,64]{0,2,1:T(8,128)(2,1)} %bitcast.246, bf16[2048,12,64]{0,2,1:T(8,128)(2,1)} %bitcast.241), kind=kOutput, calls=%fused_computation.13 | convolution fusion | flops 824177664 | bytes 29241344 | tf_op jit(solution)/shard_map/while/body/eval_jaxpr/qhd,khd->hqk/dot_general | solution.py:48
  63.7 12.4 %fusion.2 = f32[12,256]{1,0:T(8,128)} fusion(f32[12,256]{1,0:T(8,128)S(1)} %get-tuple-element.97, f32[12,256,2048]{2,1,0:T(8,128)} %get-tuple-element.98, pred[256,2048]{1,0:T(8,128)(4,1)S(1)} %copy-done.5), kind=kLoop, calls=%fused_computation.6 | loop fusion | flops 25162752 | bytes 25714688 | tf_op jit(solution)/shard_map/while/body/eval_jaxpr/reduce_sum | solution.py:63
  80.8 13.0 %fusion.136 = bf16[12,64,256]{2,1,0:T(8,128)(2,1)S(1)} fusion(bf16[2048,12,64]{0,2,1:T(8,128)(2,1)} %bitcast.244, f32[12,256]{1,0:T(8,128)} %fusion.2, f32[12,256]{1,0:T(8,128)S(1)} %get-tuple-element.97, f32[12,256,2048]{2,1,0:T(8,128)} %get-tuple-element.98, pred[256,2048]{1,0:T(8,128)(4,1)} %fusion.97), kind=kOutput, calls=%fused_computation.146 | convolution fusion | flops 836960256 | bytes 29253632 | tf_op jit(solution)/shard_map/while/body/eval_jaxpr/hqk,khd->qhd/dot_general | solution.py:66
  96.8 20.8 %all_to_all.20 = bf16[1,2,8,48,768]{4,3,1,0,2:T(8,128)(2,1)S(1)} all-to-all(bf16[1,2,8,48,768]{4,3,1,0,2:T(8,128)(2,1)S(1)} %copy.58), channel_id=1, replica_groups=mesh['dp'=16,'expert'=8] {'expert'}, dimensions={2} | all-to-all | bytes 2359296 | tf_op jit(solution)/shard_map/all_to_all | solution.py:207
  117.6 6.0 fusion.140
  123.6 10.5 fusion.14
  140.8 13.1 %fusion.126 = bf16[1,1,8,48,768]{4,3,2,1,0:T(8,128)(2,1)S(1)} fusion(bf16[1,3072,768]{2,1,0:T(8,128)(2,1)S(1)} %bitcast.293, f32[8,48,3072]{2,1,0:T(8,128)S(1)} %get-tuple-element.102, u8[48,3072]{1,0:T(8,128)(4,1)S(1)} %get-tuple-element.56, u8[48,3072]{1,0:T(8,128)(4,1)S(1)} %get-tuple-element.55), kind=kOutput, calls=%fused_computation.144 | convolution fusion | flops 1894809600 | bytes 10321920 | tf_op jit(solution)/shard_map/gnsf,fd->gnsd/dot_general | solution.py:216
  161.3 15.5 %all-to-all-done.1 = bf16[1,2,8,48,768]{4,3,1,0,2:T(8,128)(2,1)} async-done(((bf16[1,2,8,48,768]{4,3,1,0,2:T(8,128)(2,1)}), bf16[1,2,8,48,768]{4,3,1,0,2:T(8,128)(2,1)}, u32[]{:S(2)}, u32[]{:S(2)}) %all-to-all-start.1) | async-done | bytes 1179680 | tf_op jit(solution)/shard_map/all_to_all | solution.py:221
  182.1 20.6 %all_to_all.21 = bf16[1,2,8,48,768]{4,3,1,0,2:T(8,128)(2,1)S(1)} all-to-all(bf16[1,2,8,48,768]{4,3,1,0,2:T(8,128)(2,1)S(1)} %copy.63), channel_id=1, replica_groups=mesh['dp'=16,'expert'=8] {'expert'}, dimensions={2} | all-to-all | bytes 2359296 | tf_op jit(solution)/shard_map/all_to_all | solution.py:254
  202.7 5.1 fusion.26
  212.1 10.1 fusion.131
  230.3 16.0 %all-to-all-done.3 = bf16[1,2,8,48,768]{4,3,1,0,2:T(8,128)(2,1)} async-done(((bf16[1,2,8,48,768]{4,3,1,0,2:T(8,128)(2,1)}), bf16[1,2,8,48,768]{4,3,1,0,2:T(8,128)(2,1)}, u32[]{:S(2)}, u32[]{:S(2)}) %all-to-all-start.3) | async-done | bytes 1179680 | tf_op jit(solution)/shard_map/all_to_all | solution.py:276
  254.9 12.9 %fusion.62 = bf16[12,64,2048]{2,1,0:T(8,128)(2,1)} fusion(bf16[256,12,64]{0,2,1:T(8,128)(2,1)} %bitcast.251, f32[12,256]{1,0:T(8,128)S(1)} %copy-done.22, f32[12,256,2048]{2,1,0:T(8,128)} %get-tuple-element.98, pred[256,2048]{1,0:T(8,128)(4,1)} %fusion.97), kind=kOutput, calls=%fused_computation.92 | convolution fusion | flops 832045056 | bytes 29241344 | tf_op jit(solution)/shard_map/while/body/eval_jaxpr/hqk,qhd->khd/dot_general | solution.py:109
  267.9 19.9 %multiply_reduce_fusion = (f32[12,256]{1,0:T(8,128)}, f32[12,256,2048]{2,1,0:T(8,128)}) fusion(f32[12,256]{1,0:T(8,128)S(1)} %copy-done.22, f32[12,256,2048]{2,1,0:T(8,128)} %get-tuple-element.98, pred[256,2048]{1,0:T(8,128)(4,1)} %fusion.97, bf16[256,12,64]{0,2,1:T(8,128)(2,1)} %bitcast.252, bf16[2048,12,64]{0,2,1:T(8,128)(2,1)} %bitcast.245), kind=kOutput, calls=%fused_computation.1 | convolution fusion | flops 836760576 | bytes 54419456 | tf_op jit(solution)/shard_map/while/body/eval_jaxpr/qhd,khd->hqk/dot_general | solution.py:83
  287.8 18.0 %multiply_convert_fusion = bf16[12,256,2048]{2,1,0:T(8,128)(2,1)S(1)} fusion(f32[12,256,2048]{2,1,0:T(8,128)} %get-tuple-element.105, f32[12,256]{1,0:T(8,128)} %get-tuple-element.104, f32[12,256]{1,0:T(8,128)S(1)} %copy-done.22, f32[12,256,2048]{2,1,0:T(8,128)} %get-tuple-element.98, pred[256,2048]{1,0:T(8,128)(4,1)} %fusion.97), kind=kLoop, calls=%fused_computation | loop fusion | flops 37748736 | bytes 63463424 | tf_op jit(solution)/shard_map/while/body/eval_jaxpr/convert_element_type | solution.py:87
  311.6 6.7 fusion.55
  318.4 6.9 fusion.56
  328.6 9.4 fusion.125
  338.0 8.6 reduce-scatter.9.cloned.1.call-done
  346.7 5.5 fusion.164
  352.2 373.4 %fusion.245 = (f32[8,2304]{1,0:T(8,128)}, f32[8,768]{1,0:T(8,128)}) fusion(f32[768,2304]{1,0:T(8,128)} %fusion.164, f32[768,768]{1,0:T(8,128)} %fusion.170), kind=kCustom, calls=%all-reduce-scatter.2 | all-reduce-scatter fusion | flops 3145729 | bytes 9535488
  743.3 12.9 %collective-permute-start.54 = (f32[8,768]{1,0:T(8,128)}, f32[8,768]{1,0:T(8,128)}, u32[]{:S(2)}, u32[]{:S(2)}) collective-permute-start(f32[8,768]{1,0:T(8,128)} %get-tuple-element.86), channel_id=1, source_target_pairs={{0,23},{1,24},{2,25},{3,26},{4,27},{5,28},{6,29},{7,30},{8,31},{9,... | collective-permute-start | bytes 73736
  764.8 4.7 collective-permute-start.49
  804.5 4.8 collective-permute-start.35
  867.6 5.0 collective-permute-start.11
  875.7 64.6 %all-reduce.7 = (f32[768]{0:T(1024)S(1)}, f32[768]{0:T(1024)S(1)}, f32[768,16]{1,0:T(8,128)}) all-reduce(f32[768]{0:T(1024)} %get-tuple-element.61, f32[768]{0:T(1024)S(1)} %copy-done.52, f32[768,16]{1,0:T(8,128)} %fusion.189), channel_id=4, replica_groups=mesh['dp'=16,'expert'=8] {'dp','expert'}, use_global_device_ids=true, to_apply=%region_22.23.clone | all-reduce | flops 13824 | bytes 110592
  944.2 4.7 collective-permute-start.8
  961.4 47.2 %concatenate.23 = f32[262,768]{1,0:T(8,128)} concatenate(f32[6,768]{1,0:T(8,128)} %copy-done.38, f32[8,768]{1,0:T(8,128)} %collective-permute-done.62, f32[8,768]{1,0:T(8,128)} %collective-permute-done.61, f32[8,768]{1,0:T(8,128)} %collective-permute-done.60, f32[8,768]{1,0:T(8,128)} %collective-permute-done.59, f32[8,768]{1,0:T(8,128)} %collective-permute-done.58, ...), dimensions={0} | concatenate | bytes 1609728
  1011.2 5.5 collective-permute-start.3
  1025.1 54.1 %concatenate.22 = f32[262,2304]{1,0:T(8,128)} concatenate(f32[6,2304]{1,0:T(8,128)} %copy-done.25, f32[8,2304]{1,0:T(8,128)} %copy-done.24, f32[8,2304]{1,0:T(8,128)} %collective-permute-done.29, f32[8,2304]{1,0:T(8,128)} %collective-permute-done.28, f32[8,2304]{1,0:T(8,128)} %collective-permute-done.27, f32[8,2304]{1,0:T(8,128)} %copy-done.26, ...), dimensions={0} | concatenate | bytes 4829184
  (389 shorter events, 228.7 us)
Async XLA Ops:
  7.2 36.4 %all-gather.5.cloned.1.call-start = ((), (), s32[]{:S(2)}) async-start(), calls=%async_computation.9 | async-start | bytes 3538944 | tf_op jit(solution)/shard_map/all_gather | solution.py:181
  13.0 63.0 %all-gather.3.cloned.1.call-start = ((), (), s32[]{:S(2)}) async-start(), calls=%async_computation.8 | async-start | bytes 3538944 | tf_op jit(solution)/shard_map/all_gather | solution.py:182
  155.2 21.6 %all-to-all-start.1 = ((bf16[1,2,8,48,768]{4,3,1,0,2:T(8,128)(2,1)}), bf16[1,2,8,48,768]{4,3,1,0,2:T(8,128)(2,1)}, u32[]{:S(2)}, u32[]{:S(2)}) async-start(bf16[1,2,8,48,768]{4,3,1,0,2:T(8,128)(2,1)} %copy.61), calls=%async_computation.1 | async-start | bytes 2359296 | tf_op jit(solution)/shard_map/all_to_all | solution.py:221
  224.7 21.6 %all-to-all-start.3 = ((bf16[1,2,8,48,768]{4,3,1,0,2:T(8,128)(2,1)}), bf16[1,2,8,48,768]{4,3,1,0,2:T(8,128)(2,1)}, u32[]{:S(2)}, u32[]{:S(2)}) async-start(bf16[1,2,8,48,768]{4,3,1,0,2:T(8,128)(2,1)} %copy.66), calls=%async_computation.3 | async-start | bytes 2359296 | tf_op jit(solution)/shard_map/all_to_all | solution.py:276
  228.9 109.1 %reduce-scatter.11.cloned.1.call-start = ((), (), s32[]{:S(2)}) async-start(), calls=%async_computation.11 | async-start | bytes 3538944 | tf_op jit(solution)/shard_map/reduce_scatter | solution.py:312
  267.9 78.8 %reduce-scatter.9.cloned.1.call-start = ((), (), s32[]{:S(2)}) async-start(), calls=%async_computation.10 | async-start | bytes 3538944 | tf_op jit(solution)/shard_map/reduce_scatter | solution.py:309
  311.4 769.3 %reduce-scatter.13.cloned.1.call-start = ((), (), s32[]{:S(2)}) async-start(), calls=%async_computation.12 | async-start | bytes 5013504 | tf_op jit(solution)/shard_map/reduce_scatter | solution.py:141
  318.3 764.2 %reduce-scatter.15.cloned.1.call-start = ((), (), s32[]{:S(2)}) async-start(), calls=%async_computation.13 | async-start | bytes 5013504 | tf_op jit(solution)/shard_map/reduce_scatter | solution.py:144
  735.8 20.5 %collective-permute-start.58 = (f32[8,768]{1,0:T(8,128)}, f32[8,768]{1,0:T(8,128)}, u32[]{:S(2)}, u32[]{:S(2)}) collective-permute-start(f32[8,768]{1,0:T(8,128)} %get-tuple-element.86), channel_id=1, source_target_pairs={{0,27},{1,28},{2,29},{3,30},{4,31},{5,32},{6,33},{7,34},{8,35},{9,... | collective-permute-start | bytes 73736
  737.7 21.1 %collective-permute-start.57 = (f32[8,768]{1,0:T(8,128)}, f32[8,768]{1,0:T(8,128)}, u32[]{:S(2)}, u32[]{:S(2)}) collective-permute-start(f32[8,768]{1,0:T(8,128)} %get-tuple-element.86), channel_id=1, source_target_pairs={{0,26},{1,27},{2,28},{3,29},{4,30},{5,31},{6,32},{7,33},{8,34},{9,... | collective-permute-start | bytes 73736
  739.5 21.1 %collective-permute-start.56 = (f32[8,768]{1,0:T(8,128)}, f32[8,768]{1,0:T(8,128)}, u32[]{:S(2)}, u32[]{:S(2)}) collective-permute-start(f32[8,768]{1,0:T(8,128)} %get-tuple-element.86), channel_id=1, source_target_pairs={{0,25},{1,26},{2,27},{3,28},{4,29},{5,30},{6,31},{7,32},{8,33},{9,... | collective-permute-start | bytes 73736
  741.4 21.5 %collective-permute-start.55 = (f32[8,768]{1,0:T(8,128)}, f32[8,768]{1,0:T(8,128)}, u32[]{:S(2)}, u32[]{:S(2)}) collective-permute-start(f32[8,768]{1,0:T(8,128)} %get-tuple-element.86), channel_id=1, source_target_pairs={{0,24},{1,25},{2,26},{3,27},{4,28},{5,29},{6,30},{7,31},{8,32},{9,... | collective-permute-start | bytes 73736
  743.3 21.5 %collective-permute-start.54 = (f32[8,768]{1,0:T(8,128)}, f32[8,768]{1,0:T(8,128)}, u32[]{:S(2)}, u32[]{:S(2)}) collective-permute-start(f32[8,768]{1,0:T(8,128)} %get-tuple-element.86), channel_id=1, source_target_pairs={{0,23},{1,24},{2,25},{3,26},{4,27},{5,28},{6,29},{7,30},{8,31},{9,... | collective-permute-start | bytes 73736
  784.1 15.9 %collective-permute-start.42 = (f32[8,768]{1,0:T(8,128)}, f32[8,768]{1,0:T(8,128)S(1)}, u32[]{:S(2)}, u32[]{:S(2)}) collective-permute-start(f32[8,768]{1,0:T(8,128)} %get-tuple-element.86), channel_id=1, source_target_pairs={{0,11},{1,12},{2,13},{3,14},{4,15},{5,16},{6,17},{7,18},{8,19},{9,... | collective-permute-start | bytes 73736
  785.4 16.5 %collective-permute-start.41 = (f32[8,768]{1,0:T(8,128)}, f32[8,768]{1,0:T(8,128)S(1)}, u32[]{:S(2)}, u32[]{:S(2)}) collective-permute-start(f32[8,768]{1,0:T(8,128)} %get-tuple-element.86), channel_id=1, source_target_pairs={{0,10},{1,11},{2,12},{3,13},{4,14},{5,15},{6,16},{7,17},{8,18},{9,... | collective-permute-start | bytes 73736
  787.0 17.4 %collective-permute-start.40 = (f32[8,768]{1,0:T(8,128)}, f32[8,768]{1,0:T(8,128)S(1)}, u32[]{:S(2)}, u32[]{:S(2)}) collective-permute-start(f32[8,768]{1,0:T(8,128)} %get-tuple-element.86), channel_id=1, source_target_pairs={{0,9},{1,10},{2,11},{3,12},{4,13},{5,14},{6,15},{7,16},{8,17},{9,1... | collective-permute-start | bytes 73736
  793.0 19.3 %collective-permute-start.39 = (f32[8,768]{1,0:T(8,128)}, f32[8,768]{1,0:T(8,128)S(1)}, u32[]{:S(2)}, u32[]{:S(2)}) collective-permute-start(f32[8,768]{1,0:T(8,128)} %get-tuple-element.86), channel_id=1, source_target_pairs={{0,8},{1,9},{2,10},{3,11},{4,12},{5,13},{6,14},{7,15},{8,16},{9,17... | collective-permute-start | bytes 73736
  796.0 17.8 %collective-permute-start.38 = (f32[8,768]{1,0:T(8,128)}, f32[8,768]{1,0:T(8,128)S(1)}, u32[]{:S(2)}, u32[]{:S(2)}) collective-permute-start(f32[8,768]{1,0:T(8,128)} %get-tuple-element.86), channel_id=1, source_target_pairs={{0,7},{1,8},{2,9},{3,10},{4,11},{5,12},{6,13},{7,14},{8,15},{9,16}... | collective-permute-start | bytes 73736
  800.1 16.0 %collective-permute-start.37 = (f32[8,768]{1,0:T(8,128)}, f32[8,768]{1,0:T(8,128)S(1)}, u32[]{:S(2)}, u32[]{:S(2)}) collective-permute-start(f32[8,768]{1,0:T(8,128)} %get-tuple-element.86), channel_id=1, source_target_pairs={{0,6},{1,7},{2,8},{3,9},{4,10},{5,11},{6,12},{7,13},{8,14},{9,15},... | collective-permute-start | bytes 73736
  802.0 17.3 %collective-permute-start.36 = (f32[8,768]{1,0:T(8,128)}, f32[8,768]{1,0:T(8,128)S(1)}, u32[]{:S(2)}, u32[]{:S(2)}) collective-permute-start(f32[8,768]{1,0:T(8,128)} %get-tuple-element.86), channel_id=1, source_target_pairs={{0,5},{1,6},{2,7},{3,8},{4,9},{5,10},{6,11},{7,12},{8,13},{9,14},{... | collective-permute-start | bytes 73736
  804.5 16.1 %collective-permute-start.35 = (f32[8,768]{1,0:T(8,128)}, f32[8,768]{1,0:T(8,128)S(1)}, u32[]{:S(2)}, u32[]{:S(2)}) collective-permute-start(f32[8,768]{1,0:T(8,128)} %get-tuple-element.86), channel_id=1, source_target_pairs={{0,4},{1,5},{2,6},{3,7},{4,8},{5,9},{6,10},{7,11},{8,12},{9,13},{1... | collective-permute-start | bytes 73736
  860.5 81.0 %collective-permute-start.14 = (f32[8,2304]{1,0:T(8,128)}, f32[8,2304]{1,0:T(8,128)}, u32[]{:S(2)}, u32[]{:S(2)}) collective-permute-start(f32[8,2304]{1,0:T(8,128)} %get-tuple-element.85), channel_id=1, source_target_pairs={{0,15},{1,16},{2,17},{3,18},{4,19},{5,20},{6,21},{7,22},{8,23},{9,... | collective-permute-start | bytes 221192
  862.5 81.7 %collective-permute-start.13 = (f32[8,2304]{1,0:T(8,128)}, f32[8,2304]{1,0:T(8,128)}, u32[]{:S(2)}, u32[]{:S(2)}) collective-permute-start(f32[8,2304]{1,0:T(8,128)} %get-tuple-element.85), channel_id=1, source_target_pairs={{0,14},{1,15},{2,16},{3,17},{4,18},{5,19},{6,20},{7,21},{8,22},{9,... | collective-permute-start | bytes 221192
  865.7 83.2 %collective-permute-start.12 = (f32[8,2304]{1,0:T(8,128)}, f32[8,2304]{1,0:T(8,128)}, u32[]{:S(2)}, u32[]{:S(2)}) collective-permute-start(f32[8,2304]{1,0:T(8,128)} %get-tuple-element.85), channel_id=1, source_target_pairs={{0,13},{1,14},{2,15},{3,16},{4,17},{5,18},{6,19},{7,20},{8,21},{9,... | collective-permute-start | bytes 221192
  867.6 85.5 %collective-permute-start.11 = (f32[8,2304]{1,0:T(8,128)}, f32[8,2304]{1,0:T(8,128)}, u32[]{:S(2)}, u32[]{:S(2)}) collective-permute-start(f32[8,2304]{1,0:T(8,128)} %get-tuple-element.85), channel_id=1, source_target_pairs={{0,12},{1,13},{2,14},{3,15},{4,16},{5,17},{6,18},{7,19},{8,20},{9,... | collective-permute-start | bytes 221192
  872.6 83.8 %collective-permute-start.10 = (f32[8,2304]{1,0:T(8,128)}, f32[8,2304]{1,0:T(8,128)}, u32[]{:S(2)}, u32[]{:S(2)}) collective-permute-start(f32[8,2304]{1,0:T(8,128)} %get-tuple-element.85), channel_id=1, source_target_pairs={{0,11},{1,12},{2,13},{3,14},{4,15},{5,16},{6,17},{7,18},{8,19},{9,... | collective-permute-start | bytes 221192
  941.5 67.0 %collective-permute-start.9 = (f32[8,2304]{1,0:T(8,128)}, f32[8,2304]{1,0:T(8,128)}, u32[]{:S(2)}, u32[]{:S(2)}) collective-permute-start(f32[8,2304]{1,0:T(8,128)} %get-tuple-element.85), channel_id=1, source_target_pairs={{0,10},{1,11},{2,12},{3,13},{4,14},{5,15},{6,16},{7,17},{8,18},{9,... | collective-permute-start | bytes 221192
  944.2 67.1 %collective-permute-start.8 = (f32[8,2304]{1,0:T(8,128)}, f32[8,2304]{1,0:T(8,128)}, u32[]{:S(2)}, u32[]{:S(2)}) collective-permute-start(f32[8,2304]{1,0:T(8,128)} %get-tuple-element.85), channel_id=1, source_target_pairs={{0,9},{1,10},{2,11},{3,12},{4,13},{5,14},{6,15},{7,16},{8,17},{9,1... | collective-permute-start | bytes 221192
  948.9 67.9 %collective-permute-start.7 = (f32[8,2304]{1,0:T(8,128)}, f32[8,2304]{1,0:T(8,128)}, u32[]{:S(2)}, u32[]{:S(2)}) collective-permute-start(f32[8,2304]{1,0:T(8,128)} %get-tuple-element.85), channel_id=1, source_target_pairs={{0,8},{1,9},{2,10},{3,11},{4,12},{5,13},{6,14},{7,15},{8,16},{9,17... | collective-permute-start | bytes 221192
  953.1 65.5 %collective-permute-start.6 = (f32[8,2304]{1,0:T(8,128)}, f32[8,2304]{1,0:T(8,128)}, u32[]{:S(2)}, u32[]{:S(2)}) collective-permute-start(f32[8,2304]{1,0:T(8,128)} %get-tuple-element.85), channel_id=1, source_target_pairs={{0,7},{1,8},{2,9},{3,10},{4,11},{5,12},{6,13},{7,14},{8,15},{9,16}... | collective-permute-start | bytes 221192
  956.3 64.4 %collective-permute-start.5 = (f32[8,2304]{1,0:T(8,128)}, f32[8,2304]{1,0:T(8,128)}, u32[]{:S(2)}, u32[]{:S(2)}) collective-permute-start(f32[8,2304]{1,0:T(8,128)} %get-tuple-element.85), channel_id=1, source_target_pairs={{0,6},{1,7},{2,8},{3,9},{4,10},{5,11},{6,12},{7,13},{8,14},{9,15},... | collective-permute-start | bytes 221192
  1008.5 16.5 %collective-permute-start.4 = (f32[8,2304]{1,0:T(8,128)}, f32[8,2304]{1,0:T(8,128)}, u32[]{:S(2)}, u32[]{:S(2)}) collective-permute-start(f32[8,2304]{1,0:T(8,128)} %get-tuple-element.85), channel_id=1, source_target_pairs={{0,5},{1,6},{2,7},{3,8},{4,9},{5,10},{6,11},{7,12},{8,13},{9,14},{... | collective-permute-start | bytes 221192
  (126 other events, 2503.9 us)
Sparse Core Ops, SparseCore 0:
  13.2 30.4 all-gather.4
  45.9 27.8 all-gather.2
  268.0 35.1 reduce-scatter.10
  311.5 35.1 reduce-scatter.8
  349.9 78.1 reduce-scatter.12
  431.3 78.7 reduce-scatter.14
where the time goes:
time: 1110 us; the launch traced here: 1090 us
  blocking collectives  479 us (43%)
  starting transfers between devices  180 us (16%)
  matrix products  160 us (14%)
  local copies, waits for them, and re-layouts  138 us (12%)
  waiting for transfers between devices  59.6 us (5%)
  other arithmetic  58.6 us (5%)
  between operations  16.6 us (1%)
    unnamed x2, blocking collectives  438 us
    unnamed x64, starting transfers between devices  171 us
    unnamed x181, local copies, waits for them, and re-layouts  116 us
  transfers between devices with their start and end apart: 72, of which 4 were waited for; matrix products, arithmetic and copies ran while one was open for 56% of the time, Pallas kernels for 0%

commit v1 on v0

--- a/solution.py
+++ b/solution.py
@@ -330,12 +330,22 @@
     norm1_gain_grad = jnp.sum(grad_hidden_one * normed_one, axis=(0, 1))
     tokens_grad = grad_residual + norm_back(grad_hidden_one * norm1_gain, normed_one, inverse_one)
     expert_sums = sum_experts(new_in_grad, new_out_grad)
+    everyone = lax.axis_size("dp") * count
+    own = width // everyone
+    matrices = jnp.concatenate([qkv_grad, proj_grad], axis=1).reshape(everyone, own, -1)
+    matrices = lax.psum_scatter(matrices, ("dp", "expert"), scatter_dimension=0, tiled=True)[0]
+    narrow = jnp.concatenate(
+        [router_grad, norm1_gain_grad[:, None], norm2_gain_grad[:, None]], axis=1
+    )
+    narrow = lax.psum(narrow, ("dp", "expert"))
+    first_row = (lax.axis_index("dp") * count + lax.axis_index("expert")) * own
+    narrow = lax.dynamic_slice_in_dim(narrow, first_row, own, axis=0)
     dense_sums = (
-        lax.psum_scatter(norm1_gain_grad, ("dp", "expert"), scatter_dimension=0, tiled=True),
-        lax.psum_scatter(qkv_grad, ("dp", "expert"), scatter_dimension=0, tiled=True),
-        lax.psum_scatter(proj_grad, ("dp", "expert"), scatter_dimension=0, tiled=True),
-        lax.psum_scatter(norm2_gain_grad, ("dp", "expert"), scatter_dimension=0, tiled=True),
-        lax.psum_scatter(router_grad, ("dp", "expert"), scatter_dimension=0, tiled=True),
+        narrow[:, -2],
+        matrices[:, : 3 * width],
+        matrices[:, 3 * width :],
+        narrow[:, -1],
+        narrow[:, :-2],
     )
     return (
         mixed,

time: 1110 us -> 755 us (0.68)
  blocking collectives: 479 us -> 107 us
  waiting for transfers between devices: 59.6 us -> 335 us
  starting transfers between devices: 180 us -> 9.06 us
  local copies, waits for them, and re-layouts: 138 us -> 45.4 us
  other arithmetic: 58.6 us -> 71.3 us
    unnamed x2 -> x0, blocking collectives: 438 us -> none
    reduce_scatter x0 -> x1, waiting for transfers between devices: none -> 224 us  [on_device(): lax.psum_scatter(matrices, ('dp', 'expert'), scatter_dimension=0, tiled=T...]
    unnamed x64 -> x0, starting transfers between devices: 171 us -> none
    unnamed x181 -> x131, local copies, waits for them, and re-layouts: 116 us -> 7.75 us
    psum x0 -> x1, blocking collectives: none -> 66.3 us  [on_device(): narrow = lax.psum(narrow, ('dp', 'expert'))]
    reduce_scatter x1, waiting for transfers between devices: 0.01 us -> 50.9 us  [sum_experts(): lax.psum_scatter(out_grad_weights[None].astype(jnp.bfloat16), 'dp', scatt...]
  transfers between devices with their start and end apart: 72 -> 9, of which waited for: 4 -> 6; matrix products, arithmetic and copies ran while one was open for 56% -> 21% of each run, Pallas kernels for 0% -> 0%
where the time goes in v1:
time: 755 us; the launch traced here: 744 us
  waiting for transfers between devices  335 us (44%)
  matrix products  160 us (21%)
  blocking collectives  107 us (14%)
  other arithmetic  71.3 us (9%)
  local copies, waits for them, and re-layouts  45.4 us (6%)
  between operations  16.1 us (2%)
  starting transfers between devices  9.06 us (1%)
    reduce_scatter x1, waiting for transfers between devices, on_device(): lax.psum_scatter(matrices, ('dp', 'expert'), scatter_dimension=0, tiled=T...  224 us
    psum x1, blocking collectives, on_device(): narrow = lax.psum(narrow, ('dp', 'expert'))  66.3 us
    reduce_scatter x1, waiting for transfers between devices, sum_experts(): lax.psum_scatter(out_grad_weights[None].astype(jnp.bfloat16), 'dp', scatt...  50.9 us
    all_to_all x1, blocking collectives, on_device(): lax.all_to_all(buffers, 'expert', split_axis=2, concat_axis=2, tiled=True)  20.8 us
    all_to_all x1, blocking collectives, on_device(): lax.all_to_all(grad_returned, 'expert', split_axis=2, concat_axis=2, tile...  20.3 us
    dot_general x1, matrix products, query_part(): jnp.einsum('qhd,khd->hqk', grad_heads, value_heads, preferred_element_typ...  19.8 us
    all_gather x1, waiting for transfers between devices, on_device(): lax.all_gather(keys_local, 'expert', axis=1, tiled=True)  18.5 us
    convert_element_type x1, other arithmetic, query_part(): grad_scores = (probs * (grad_probs - row_delta)).astype(jnp.bfloat16)  18 us
  transfers between devices with their start and end apart: 9, of which 6 were waited for; matrix products, arithmetic and copies ran while one was open for 21% of the time, Pallas kernels for 0%

profile of v1, /device:TPU:0, one launch (start us, length us, event | category | flops | bytes accessed | tf_op | source)
XLA Modules:
  0.0 744.3 jit_solution(11227667822750820822)
XLA Ops:
  25.1 18.5 %all-gather.5.cloned.1.call-done = bf16[1,2048,768]{2,1,0:T(8,128)(2,1)} async-done(((bf16[1,256,768]{2,1,0:T(8,128)(2,1)}), bf16[1,2048,768]{2,1,0:T(8,128)(2,1)}) %all-gather.5.cloned.1.call-update) | async-done | bytes 3145744 | tf_op jit(solution)/shard_map/all_gather | solution.py:181
  43.6 4.7 copy.60
  48.3 15.3 %fusion.6 = (f32[12,256]{1,0:T(8,128)S(1)}, f32[12,256,2048]{2,1,0:T(8,128)}) fusion(pred[256,2048]{1,0:T(8,128)(4,1)} %fusion.95, bf16[256,12,64]{0,2,1:T(8,128)(2,1)} %bitcast.251, bf16[2048,12,64]{0,2,1:T(8,128)(2,1)} %bitcast.246), kind=kOutput, calls=%fused_computation.14 | convolution fusion | flops 824177664 | bytes 29241344 | tf_op jit(solution)/shard_map/while/body/eval_jaxpr/qhd,khd->hqk/dot_general | solution.py:48
  63.6 12.4 %fusion = f32[12,256]{1,0:T(8,128)} fusion(f32[12,256]{1,0:T(8,128)S(1)} %get-tuple-element.128, f32[12,256,2048]{2,1,0:T(8,128)} %get-tuple-element.129, pred[256,2048]{1,0:T(8,128)(4,1)S(1)} %copy-done.5), kind=kLoop, calls=%fused_computation.6 | loop fusion | flops 25162752 | bytes 25714688 | tf_op jit(solution)/shard_map/while/body/eval_jaxpr/reduce_sum | solution.py:63
  76.0 4.7 copy.58
  80.7 13.0 %fusion.134 = bf16[12,64,256]{2,1,0:T(8,128)(2,1)S(1)} fusion(bf16[2048,12,64]{0,2,1:T(8,128)(2,1)} %bitcast.249, f32[12,256]{1,0:T(8,128)} %fusion, f32[12,256]{1,0:T(8,128)S(1)} %get-tuple-element.128, f32[12,256,2048]{2,1,0:T(8,128)} %get-tuple-element.129, pred[256,2048]{1,0:T(8,128)(4,1)} %fusion.95), kind=kOutput, calls=%fused_computation.147 | convolution fusion | flops 836960256 | bytes 29253632 | tf_op jit(solution)/shard_map/while/body/eval_jaxpr/hqk,khd->qhd/dot_general | solution.py:66
  96.8 20.8 %all_to_all.20 = bf16[1,2,8,48,768]{4,3,1,0,2:T(8,128)(2,1)S(1)} all-to-all(bf16[1,2,8,48,768]{4,3,1,0,2:T(8,128)(2,1)S(1)} %copy.64), channel_id=1, replica_groups=mesh['dp'=16,'expert'=8] {'expert'}, dimensions={2} | all-to-all | bytes 2359296 | tf_op jit(solution)/shard_map/all_to_all | solution.py:207
  117.6 6.0 fusion.138
  123.6 10.5 %fusion.12 = bf16[8,48,3072]{2,1,0:T(8,128)(2,1)S(1)} fusion(f32[8,48,3072]{2,1,0:T(8,128)S(1)} %get-tuple-element.132, u8[48,3072]{1,0:T(8,128)(4,1)S(1)} %get-tuple-element.105, u8[48,3072]{1,0:T(8,128)(4,1)S(1)} %get-tuple-element.104), kind=kLoop, calls=%fused_computation.25 | loop fusion | flops 82575360 | bytes 7372800 | tf_op jit(solution)/shard_map/convert_element_type | solution.py:215
  140.6 13.3 %fusion.124 = bf16[1,1,8,48,768]{4,3,2,1,0:T(8,128)(2,1)S(1)} fusion(bf16[1,3072,768]{2,1,0:T(8,128)(2,1)S(1)} %bitcast.300, f32[8,48,3072]{2,1,0:T(8,128)S(1)} %get-tuple-element.133, u8[48,3072]{1,0:T(8,128)(4,1)S(1)} %get-tuple-element.103, u8[48,3072]{1,0:T(8,128)(4,1)S(1)} %get-tuple-element.102), kind=kOutput, calls=%fused_computation.145 | convolution fusion | flops 1894809600 | bytes 10321920 | tf_op jit(solution)/shard_map/gnsf,fd->gnsd/dot_general | solution.py:216
  155.3 4.3 all-to-all-start.1
  161.4 15.5 %all-to-all-done.1 = bf16[1,2,8,48,768]{4,3,1,0,2:T(8,128)(2,1)} async-done(((bf16[1,2,8,48,768]{4,3,1,0,2:T(8,128)(2,1)}), bf16[1,2,8,48,768]{4,3,1,0,2:T(8,128)(2,1)}, u32[]{:S(2)}, u32[]{:S(2)}) %all-to-all-start.1) | async-done | bytes 1179680 | tf_op jit(solution)/shard_map/all_to_all | solution.py:221
  182.2 20.3 %all_to_all.21 = bf16[1,2,8,48,768]{4,3,1,0,2:T(8,128)(2,1)S(1)} all-to-all(bf16[1,2,8,48,768]{4,3,1,0,2:T(8,128)(2,1)S(1)} %copy.69), channel_id=1, replica_groups=mesh['dp'=16,'expert'=8] {'expert'}, dimensions={2} | all-to-all | bytes 2359296 | tf_op jit(solution)/shard_map/all_to_all | solution.py:254
  202.6 5.1 fusion.24
  212.0 10.1 %fusion.129 = bf16[1,1,8,48,768]{4,3,2,1,0:T(8,128)(2,1)} fusion(bf16[1,768,3072]{2,1,0:T(8,128)(2,1)} %param.21, f32[8,48,3072]{2,1,0:T(8,128)} %copy-done.54, bf16[1,3072,768]{2,1,0:T(8,128)(2,1)} %param.22, bf16[1,2,8,48,768]{4,3,1,0,2:T(8,128)(2,1)} %copy-done.17), kind=kOutput, calls=%fused_computation.146 | convolution fusion | flops 3635970048 | bytes 15335424 | tf_op jit(solution)/shard_map/gnsf,df->gnsd/dot_general | solution.py:269
  224.6 4.3 all-to-all-start.3
  230.3 16.0 %all-to-all-done.3 = bf16[1,2,8,48,768]{4,3,1,0,2:T(8,128)(2,1)} async-done(((bf16[1,2,8,48,768]{4,3,1,0,2:T(8,128)(2,1)}), bf16[1,2,8,48,768]{4,3,1,0,2:T(8,128)(2,1)}, u32[]{:S(2)}, u32[]{:S(2)}) %all-to-all-start.3) | async-done | bytes 1179680 | tf_op jit(solution)/shard_map/all_to_all | solution.py:276
  254.9 12.9 %fusion.60 = bf16[12,64,2048]{2,1,0:T(8,128)(2,1)} fusion(bf16[256,12,64]{0,2,1:T(8,128)(2,1)} %bitcast.256, f32[12,256]{1,0:T(8,128)S(1)} %copy-done.20, f32[12,256,2048]{2,1,0:T(8,128)} %get-tuple-element.129, pred[256,2048]{1,0:T(8,128)(4,1)} %fusion.95), kind=kOutput, calls=%fused_computation.93 | convolution fusion | flops 832045056 | bytes 29241344 | tf_op jit(solution)/shard_map/while/body/eval_jaxpr/hqk,qhd->khd/dot_general | solution.py:109
  267.9 19.8 %multiply_reduce_fusion = (f32[12,256]{1,0:T(8,128)}, f32[12,256,2048]{2,1,0:T(8,128)}) fusion(f32[12,256]{1,0:T(8,128)S(1)} %copy-done.20, f32[12,256,2048]{2,1,0:T(8,128)} %get-tuple-element.129, pred[256,2048]{1,0:T(8,128)(4,1)} %fusion.95, bf16[256,12,64]{0,2,1:T(8,128)(2,1)} %bitcast.257, bf16[2048,12,64]{0,2,1:T(8,128)(2,1)} %bitcast.250), kind=kOutput, calls=%fused_computation.1 | convolution fusion | flops 836760576 | bytes 54419456 | tf_op jit(solution)/shard_map/while/body/eval_jaxpr/qhd,khd->hqk/dot_general | solution.py:83
  287.8 18.0 %multiply_convert_fusion = bf16[12,256,2048]{2,1,0:T(8,128)(2,1)S(1)} fusion(f32[12,256,2048]{2,1,0:T(8,128)} %get-tuple-element.136, f32[12,256]{1,0:T(8,128)} %get-tuple-element.135, f32[12,256]{1,0:T(8,128)S(1)} %copy-done.20, f32[12,256,2048]{2,1,0:T(8,128)} %get-tuple-element.129, pred[256,2048]{1,0:T(8,128)(4,1)} %fusion.95), kind=kLoop, calls=%fused_computation | loop fusion | flops 37748736 | bytes 63463424 | tf_op jit(solution)/shard_map/while/body/eval_jaxpr/convert_element_type | solution.py:87
  305.8 4.7 multiply_convert_fusion.1
  311.7 6.7 fusion.53
  318.5 6.9 fusion.54
  328.8 9.4 %fusion.123 = bf16[12,64,256]{2,1,0:T(8,128)(2,1)} fusion(bf16[2048,12,64]{0,2,1:T(8,128)(2,1)S(1)} %bitcast.247, bf16[12,256,2048]{2,1,0:T(8,128)(2,1)} %copy-done.1), kind=kOutput, calls=%fused_computation.144 | convolution fusion | flops 805699584 | bytes 16121856 | tf_op jit(solution)/shard_map/while/body/eval_jaxpr/hqk,khd->qhd/dot_general | solution.py:89
  338.2 8.5 %reduce-scatter.6.cloned.1.call-done = bf16[1,256,768]{1,2,0:T(8,128)(2,1)} async-done(((bf16[1,2048,768]{1,2,0:T(8,128)(2,1)}), bf16[1,256,768]{1,2,0:T(8,128)(2,1)}) %reduce-scatter.6.cloned.1.call-update) | async-done | bytes 393232 | tf_op jit(solution)/shard_map/reduce_scatter | solution.py:309
  346.7 5.5 fusion.162
  352.2 8.7 %pad_maximum_fusion = f32[768,3072]{1,0:T(8,128)} fusion(f32[768,768]{1,0:T(8,128)} %fusion.168, f32[768,2304]{1,0:T(8,128)} %fusion.162), kind=kLoop, calls=%fused_computation.11 | loop fusion | flops 2359296 | bytes 18874368 | tf_op jit(solution)/shard_map/concatenate | solution.py:335
  360.9 10.3 %reshape.1513 = f32[128,6,3072]{2,1,0:T(8,128)} reshape(f32[768,3072]{1,0:T(8,128)} %pad_maximum_fusion) | data formatting | bytes 18874368 | tf_op jit(solution)/shard_map/reshape | solution.py:335
  376.8 4.0 fusion.150
  381.4 66.3 %psum.7 = f32[768,18]{0,1:T(8,128)} all-reduce(f32[768,18]{0,1:T(8,128)} %pad_maximum_fusion.3), channel_id=1, replica_groups=mesh['dp'=16,'expert'=8] {'dp','expert'}, use_global_device_ids=true, to_apply=%region_23.24 | all-reduce | flops 13824 | bytes 110592 | tf_op jit(solution)/shard_map/psum | solution.py:340
  457.1 50.9 %reduce-scatter.14.cloned.1.call-done = bf16[1,192,768]{2,1,0:T(8,128)(2,1)} async-done(((bf16[1,3072,768]{2,1,0:T(8,128)(2,1)}), bf16[1,192,768]{2,1,0:T(8,128)(2,1)}) %reduce-scatter.14.cloned.1.call-update) | async-done | bytes 294928 | tf_op jit(solution)/shard_map/reduce_scatter | solution.py:144
  509.8 224.4 %reduce-scatter.10.cloned.1.call-done = f32[1,6,3072]{2,1,0:T(8,128)} async-done(((f32[128,6,3072]{2,1,0:T(8,128)}), f32[1,6,3072]{2,1,0:T(8,128)}) %reduce-scatter.10.cloned.1.call-update) | async-done | bytes 73744 | tf_op jit(solution)/shard_map/reduce_scatter | solution.py:336
  (222 shorter events, 76.4 us)
Async XLA Ops:
  7.2 36.4 %all-gather.5.cloned.1.call-start = ((), (), s32[]{:S(2)}) async-start(), calls=%async_computation.10 | async-start | bytes 3538944 | tf_op jit(solution)/shard_map/all_gather | solution.py:181
  8.5 5.9 copy-start.40
  13.0 63.0 %all-gather.3.cloned.1.call-start = ((), (), s32[]{:S(2)}) async-start(), calls=%async_computation.9 | async-start | bytes 3538944 | tf_op jit(solution)/shard_map/all_gather | solution.py:182
  48.3 15.3 %copy-start.5 = (pred[256,2048]{1,0:T(8,128)(4,1)S(1)}, pred[256,2048]{1,0:T(8,128)(4,1)}, u32[]{:S(2)}) copy-start(pred[256,2048]{1,0:T(8,128)(4,1)} %fusion.95) | copy-start | bytes 1572868
  80.7 13.1 %copy-start.7 = (bf16[1,256,768]{2,1,0:T(8,128)(2,1)S(1)}, bf16[1,256,768]{2,1,0:T(8,128)(2,1)}, u32[]{:S(2)}) copy-start(bf16[1,256,768]{2,1,0:T(8,128)(2,1)} %param.13) | copy-start | bytes 1179652
  80.7 13.1 %copy-start.10 = (bf16[768,768]{1,0:T(8,128)(2,1)S(1)}, bf16[768,768]{1,0:T(8,128)(2,1)}, u32[]{:S(2)}) copy-start(bf16[768,768]{1,0:T(8,128)(2,1)} %param.18) | copy-start | bytes 3538948
  80.7 14.6 %copy-start.22 = (f32[768]{0:T(1024)S(1)}, f32[768]{0:T(1024)}, u32[]{:S(2)}) copy-start(f32[768]{0:T(1024)} %param.19) | copy-start | bytes 9220
  93.8 23.8 %copy-start.14 = (bf16[12,64,256]{2,1,0:T(8,128)(2,1)}, bf16[12,64,256]{2,1,0:T(8,128)(2,1)S(1)}, u32[]{:S(2)}) copy-start(bf16[12,64,256]{2,1,0:T(8,128)(2,1)S(1)} %fusion.134) | copy-start | bytes 1179652
  96.8 38.7 %slice-start.2 = ((s8[4718592]{0:T(1024)(128)(4,1)}), s8[4194304]{0:T(1024)(128)(4,1)S(1)}, s32[]{:S(2)}) async-start(s8[4718592]{0:T(1024)(128)(4,1)} %bitcast.295), calls=%async_computation.18 | async-start | bytes 8388608
  117.6 19.9 %copy-start.16 = (bf16[1,2,8,48,768]{4,3,1,0,2:T(8,128)(2,1)}, bf16[1,2,8,48,768]{4,3,1,0,2:T(8,128)(2,1)S(1)}, u32[]{:S(2)}) copy-start(bf16[1,2,8,48,768]{4,3,1,0,2:T(8,128)(2,1)S(1)} %all_to_all.20) | copy-start | bytes 3538948
  117.6 17.9 %slice-start.3 = ((s8[4718592]{0:T(1024)(128)(4,1)}), s8[524288]{0:T(1024)(128)(4,1)S(1)}, s32[]{:S(2)}) async-start(s8[4718592]{0:T(1024)(128)(4,1)} %bitcast.295), calls=%async_computation.19 | async-start | bytes 1048576
  123.6 14.0 %copy-start.9 = (f32[8,48,3072]{2,1,0:T(8,128)}, f32[8,48,3072]{2,1,0:T(8,128)S(1)}, u32[]{:S(2)}) copy-start(f32[8,48,3072]{2,1,0:T(8,128)S(1)} %get-tuple-element.132) | copy-start | bytes 14155780
  123.6 14.0 %slice-start.8 = ((s8[4718592]{0:T(1024)(128)(4,1)}), s8[4194304]{0:T(1024)(128)(4,1)S(1)}, s32[]{:S(2)}) async-start(s8[4718592]{0:T(1024)(128)(4,1)} %bitcast.301), calls=%async_computation.24 | async-start | bytes 8388608
  135.5 5.1 slice-start.6
  140.6 13.4 %copy-start.54 = (f32[8,48,3072]{2,1,0:T(8,128)}, f32[8,48,3072]{2,1,0:T(8,128)S(1)}, u32[]{:S(2)}) copy-start(f32[8,48,3072]{2,1,0:T(8,128)S(1)} %get-tuple-element.133) | copy-start | bytes 14155780
  155.3 21.6 %all-to-all-start.1 = ((bf16[1,2,8,48,768]{4,3,1,0,2:T(8,128)(2,1)}), bf16[1,2,8,48,768]{4,3,1,0,2:T(8,128)(2,1)}, u32[]{:S(2)}, u32[]{:S(2)}) async-start(bf16[1,2,8,48,768]{4,3,1,0,2:T(8,128)(2,1)} %copy.67), calls=%async_computation.1 | async-start | bytes 2359296 | tf_op jit(solution)/shard_map/all_to_all | solution.py:221
  178.4 24.2 %slice-start = ((s8[4718592]{0:T(1024)(128)(4,1)}), s8[4194304]{0:T(1024)(128)(4,1)S(1)}, s32[]{:S(2)}) async-start(s8[4718592]{0:T(1024)(128)(4,1)} %bitcast.253), calls=%async_computation.16 | async-start | bytes 8388608
  181.1 21.4 %slice-start.1 = ((s8[4718592]{0:T(1024)(128)(4,1)}), s8[524288]{0:T(1024)(128)(4,1)S(1)}, s32[]{:S(2)}) async-start(s8[4718592]{0:T(1024)(128)(4,1)} %bitcast.253), calls=%async_computation.17 | async-start | bytes 1048576
  182.1 27.0 %slice-start.4 = ((s8[4718592]{0:T(1024)(128)(4,1)}), s8[4194304]{0:T(1024)(128)(4,1)S(1)}, s32[]{:S(2)}) async-start(s8[4718592]{0:T(1024)(128)(4,1)} %bitcast.297), calls=%async_computation.20 | async-start | bytes 8388608
  202.6 6.6 slice-start.5
  224.6 21.6 %all-to-all-start.3 = ((bf16[1,2,8,48,768]{4,3,1,0,2:T(8,128)(2,1)}), bf16[1,2,8,48,768]{4,3,1,0,2:T(8,128)(2,1)}, u32[]{:S(2)}, u32[]{:S(2)}) async-start(bf16[1,2,8,48,768]{4,3,1,0,2:T(8,128)(2,1)} %copy.72), calls=%async_computation.3 | async-start | bytes 2359296 | tf_op jit(solution)/shard_map/all_to_all | solution.py:276
  228.9 109.4 %reduce-scatter.8.cloned.1.call-start = ((), (), s32[]{:S(2)}) async-start(), calls=%async_computation.12 | async-start | bytes 3538944 | tf_op jit(solution)/shard_map/reduce_scatter | solution.py:312
  249.2 5.7 copy-start.20
  267.9 78.8 %reduce-scatter.6.cloned.1.call-start = ((), (), s32[]{:S(2)}) async-start(), calls=%async_computation.11 | async-start | bytes 3538944 | tf_op jit(solution)/shard_map/reduce_scatter | solution.py:309
  287.8 18.0 %copy-start.8 = (bf16[1,256,768]{1,2,0:T(8,128)(2,1)S(1)}, bf16[1,256,768]{1,2,0:T(8,128)(2,1)}, u32[]{:S(2)}) copy-start(bf16[1,256,768]{1,2,0:T(8,128)(2,1)} %copy.59) | copy-start | bytes 1179652
  305.8 5.6 copy-start.1
  311.4 143.8 %reduce-scatter.12.cloned.1.call-start = ((), (), s32[]{:S(2)}) async-start(), calls=%async_computation.14 | async-start | bytes 5013504 | tf_op jit(solution)/shard_map/reduce_scatter | solution.py:141
  318.4 189.5 %reduce-scatter.14.cloned.1.call-start = ((), (), s32[]{:S(2)}) async-start(), calls=%async_computation.15 | async-start | bytes 5013504 | tf_op jit(solution)/shard_map/reduce_scatter | solution.py:144
  325.5 408.7 %reduce-scatter.10.cloned.1.call-start = ((), (), s32[]{:S(2)}) async-start(), calls=%async_computation.13 | async-start | bytes 12681216 | tf_op jit(solution)/shard_map/reduce_scatter | solution.py:336
  328.8 17.9 %copy-start.24 = (f32[768]{0:T(1024)S(1)}, f32[768]{0:T(1024)}, u32[]{:S(2)}) copy-start(f32[768]{0:T(1024)} %param.16) | copy-start | bytes 9220
  328.8 17.9 %copy-start.34 = (f32[256]{0:T(256)S(1)}, f32[256]{0:T(256)}, u32[]{:S(2)}) copy-start(f32[256]{0:T(256)} %copy-done.33) | copy-start | bytes 3076
  328.8 17.9 %copy-start.39 = (f32[256]{0:T(256)S(1)}, f32[256]{0:T(256)}, u32[]{:S(2)}) copy-start(f32[256]{0:T(256)} %copy-done.38) | copy-start | bytes 3076
  (42 other events, 108.4 us)
Sparse Core Ops, SparseCore 0:
  13.2 30.4 all-gather.4
  45.9 27.8 all-gather.2
  268.0 35.2 reduce-scatter.7
  311.5 35.1 reduce-scatter.5
  349.9 76.9 reduce-scatter.11
  430.1 77.8 reduce-scatter.13
  513.0 221.1 reduce-scatter.9

commit v2 on v1

--- a/solution.py
+++ b/solution.py
@@ -1,6 +1,8 @@
 import jax
 import jax.numpy as jnp
 from jax import lax
+from jax.experimental import pallas as pl
+from jax.experimental.pallas import tpu as pltpu
 from jax.sharding import PartitionSpec as P
 
 HEADS = 12
@@ -32,88 +34,546 @@
     return cumulative + pre_act * density
 
 
-def mask_between(seq_kind, query_pos, key_pos):
-    half_length = LONG // 2
-    query_seq = seq_kind * (query_pos // half_length)
-    key_seq = seq_kind * (key_pos // half_length)
-    return (key_pos[None, :] <= query_pos[:, None]) & (key_seq[None, :] == query_seq[:, None])
-
-
-def masked_scores(queries, keys, seq_kind, query_start, score_scale):
-    query_rows = queries.shape[0]
-    key_rows = keys.shape[0]
-    query_heads = queries.reshape(query_rows, HEADS, HD)
-    key_heads = keys.reshape(key_rows, HEADS, HD)
-    scores = (
-        jnp.einsum("qhd,khd->hqk", query_heads, key_heads, preferred_element_type=jnp.float32)
-        * score_scale
-    )
-    query_pos = query_start + jnp.arange(query_rows, dtype=jnp.int32)
-    key_pos = jnp.arange(key_rows, dtype=jnp.int32)
-    allowed = mask_between(seq_kind, query_pos, key_pos)
-    return jnp.where(allowed[None], scores, -1e30)
-
-
-def attend_group(queries, keys_whole, values_whole, seq_kind, start_row, score_scale):
-    rows_here = queries.shape[0]
-    length = keys_whole.shape[0]
-    masked = masked_scores(queries, keys_whole, seq_kind, start_row, score_scale)
-    row_max = jnp.max(masked, axis=-1, keepdims=True)
-    exponent = jnp.exp(masked - row_max)
-    row_total = jnp.sum(exponent, axis=-1, keepdims=True)
-    probs = (exponent / row_total).astype(jnp.bfloat16)
-    value_heads = values_whole.reshape(length, HEADS, HD)
-    attended = jnp.einsum("hqk,khd->qhd", probs, value_heads, preferred_element_type=jnp.float32)
-    return (
-        attended.reshape(rows_here, HEADS * HD).astype(jnp.bfloat16),
-        row_max + jnp.log(row_total),
-    )
-
-
-def query_part(
-    queries, keys_whole, values_whole, seq_kind, start_row, score_scale, log_totals, grad_att
+MESH_ID = pl.DeviceIdType.MESH
+CHIPS = 4
+PAD = 256
+BLOCK = 256
+CHUNK = 512
+CHUNKS = LONG // CHUNK
+LOCAL_HEADS = HEADS // CHIPS
+STACK = LOCAL_HEADS * BLOCK
+NEGATIVE = -1e30
+
+
+def here():
+    position = lax.axis_index("expert")
+    return position // 2, lax.rem(position, 2)
+
+
+def device(z, core):
+    return (lax.axis_index("dp"), z * 2 + core)
+
+
+def greet(barrier):
+    position = lax.axis_index("expert")
+    for step in range(1, 8):
+        pl.semaphore_signal(
+            barrier,
+            inc=1,
+            device_id=(lax.axis_index("dp"), lax.rem(position + step, 8)),
+            device_id_type=MESH_ID,
+        )
+
+
+def push(source, target, sends, receives, index_here, index_there, where):
+    return pltpu.make_async_remote_copy(
+        src_ref=source,
+        dst_ref=target,
+        send_sem=sends.at[index_here],
+        recv_sem=receives.at[index_there],
+        device_id=where,
+        device_id_type=MESH_ID,
+    )
+
+
+def landed(region, sends, receives, index):
+    z, core = here()
+    push(region, region, sends, receives, index, index, device(z, 1 - core)).wait_recv()
+
+
+def dot_nn(left, right):
+    return jnp.dot(left, right, preferred_element_type=jnp.float32)
+
+
+def dot_nt(left, right):
+    return lax.dot_general(
+        left, right, (((1,), (1,)), ((), ())), preferred_element_type=jnp.float32
+    )
+
+
+def dot_tn(left, right):
+    return lax.dot_general(
+        left, right, (((0,), (0,)), ((), ())), preferred_element_type=jnp.float32
+    )
+
+
+def head_mask(head, value, dtype):
+    lanes = lax.broadcasted_iota(jnp.int32, (1, PAD), 1)
+    inside = (lanes >= head * HD) & (lanes < (head + 1) * HD)
+    return jnp.where(inside, value, 0.0).astype(dtype)
+
+
+def lane_tiles(values, combine):
+    result = values[:, :128]
+    for start in range(128, values.shape[1], 128):
+        result = combine(result, values[:, start : start + 128])
+    return result
+
+
+def front_kernel(
+    kind_ref,
+    tokens_ref,
+    gain_ref,
+    weight_ref,
+    hidden_ref,
+    query_ref,
+    key_ref,
+    value_ref,
+    out_ref,
+    total_ref,
+    attended_ref,
+    stacked,
+    scores,
+    largest,
+    sums,
+    acc,
+    gather_send,
+    gather_recv,
+    out_send,
+    out_recv,
 ):
-    rows_here = queries.shape[0]
-    length = keys_whole.shape[0]
-    masked = masked_scores(queries, keys_whole, seq_kind, start_row, score_scale)
-    probs = jnp.exp(masked - log_totals)
-    key_heads = keys_whole.reshape(length, HEADS, HD)
-    value_heads = values_whole.reshape(length, HEADS, HD)
-    grad_heads = grad_att.reshape(rows_here, HEADS, HD)
-    grad_probs = jnp.einsum(
-        "qhd,khd->hqk", grad_heads, value_heads, preferred_element_type=jnp.float32
-    )
-    row_delta = jnp.sum(probs * grad_probs, axis=-1, keepdims=True)
-    grad_scores = (probs * (grad_probs - row_delta)).astype(jnp.bfloat16)
-    grad_query = (
-        jnp.einsum("hqk,khd->qhd", grad_scores, key_heads, preferred_element_type=jnp.float32)
-        * score_scale
-    )
-    return (grad_query.reshape(rows_here, HEADS * HD), row_delta, probs, grad_scores)
-
-
-def attend_back(
-    queries, keys_whole, values_whole, seq_kind, start_row, score_scale, log_totals, grad_att
+    z, core = here()
+    mine = z * 2 + core
+    up, down, far = lax.rem(z + 1, CHIPS), lax.rem(z + 3, CHIPS), lax.rem(z + 2, CHIPS)
+    barrier = pltpu.get_barrier_semaphore()
+    greet(barrier)
+    normed, _ = norm_parts(tokens_ref[...].astype(jnp.float32))
+    hidden_ref[mine] = (normed * gain_ref[...]).astype(jnp.bfloat16)
+    pl.semaphore_wait(barrier, 7)
+
+    def send(region, index, where):
+        copy = push(region, region, gather_send, gather_recv, index, index, where)
+        copy.start()
+        return copy
+
+    def arrived(region, index):
+        landed(region, gather_send, gather_recv, index)
+
+    def project(block):
+        projected = dot_nn(hidden_ref[block], weight_ref[...]).astype(jnp.bfloat16)
+        query_ref[block] = projected[:, :PAD]
+        rows = pl.ds(pl.multiple_of(block * BLOCK, BLOCK), BLOCK)
+        key_ref[rows, :] = projected[:, PAD : 2 * PAD]
+        value_ref[rows, :] = projected[:, 2 * PAD :]
+
+    half = BLOCK // 2
+    first, second = pl.ds(0, half), pl.ds(half, half)
+    block_down, block_up, block_far = down * 2 + core, up * 2 + core, far * 2 + core
+    copies = [
+        send(hidden_ref.at[mine], 0, device(up, core)),
+        send(hidden_ref.at[mine], 1, device(down, core)),
+        send(hidden_ref.at[mine], 2, device(z, 1 - core)),
+    ]
+    project(mine)
+    arrived(hidden_ref.at[z * 2 + 1 - core], 2)
+    project(z * 2 + 1 - core)
+    arrived(hidden_ref.at[block_down], 0)
+    copies.append(send(hidden_ref.at[block_down, first], 3, device(up, core)))
+    copies.append(send(hidden_ref.at[block_down], 5, device(z, 1 - core)))
+    arrived(hidden_ref.at[block_up], 1)
+    copies.append(send(hidden_ref.at[block_up, second], 4, device(down, core)))
+    copies.append(send(hidden_ref.at[block_up], 6, device(z, 1 - core)))
+    project(block_down)
+    project(block_up)
+    arrived(hidden_ref.at[down * 2 + 1 - core], 5)
+    project(down * 2 + 1 - core)
+    arrived(hidden_ref.at[up * 2 + 1 - core], 6)
+    project(up * 2 + 1 - core)
+    arrived(hidden_ref.at[block_far, first], 3)
+    arrived(hidden_ref.at[block_far, second], 4)
+    copies.append(send(hidden_ref.at[block_far], 7, device(z, 1 - core)))
+    project(block_far)
+    arrived(hidden_ref.at[far * 2 + 1 - core], 7)
+    project(far * 2 + 1 - core)
+
+    kind_bias = kind_ref[0].astype(jnp.float32) * NEGATIVE
+
+    @pl.loop(0, CHIPS)
+    def _(step):
+        slot = lax.rem(z + step, CHIPS)
+        block = slot * 2 + lax.rem(core + slot, 2)
+        queries = query_ref[block]
+        for head in range(LOCAL_HEADS):
+            stacked[head * BLOCK : (head + 1) * BLOCK, :] = queries * head_mask(
+                head, HD ** (-0.5), jnp.bfloat16
+            )
+
+        def chunk_rows(chunk):
+            return pl.ds(pl.multiple_of(chunk * CHUNK, CHUNK), CHUNK)
+
+        def bias_of(chunk):
+            return jnp.where((slot >= 2) & (chunk < 2), kind_bias, 0.0)
+
+        masked = dot_nt(stacked[...], key_ref[chunk_rows(slot), :])
+        row = lax.broadcasted_iota(jnp.int32, (BLOCK, CHUNK), 0)
+        column = lax.broadcasted_iota(jnp.int32, (BLOCK, CHUNK), 1)
+        allowed = column - row <= (block - 2 * slot) * BLOCK
+        for head in range(LOCAL_HEADS):
+            part = slice(head * BLOCK, (head + 1) * BLOCK)
+            values = jnp.where(allowed, masked[part], NEGATIVE)
+            scores[slot, part, :] = values
+            largest[part, :] = lane_tiles(values, jnp.maximum)
+
+        @pl.loop(0, slot)
+        def _(chunk):
+            values = dot_nt(stacked[...], key_ref[chunk_rows(chunk), :])
+            scores[chunk] = values
+            largest[...] = jnp.maximum(
+                largest[...], lane_tiles(values, jnp.maximum) + bias_of(chunk)
+            )
+
+        row_max = jnp.max(largest[...], axis=1, keepdims=True)
+        largest[...] = jnp.broadcast_to(row_max, largest.shape)
+        sums[...] = jnp.zeros_like(sums)
+        acc[...] = jnp.zeros_like(acc)
+
+        @pl.loop(0, slot + 1)
+        def _(chunk):
+            exponent = jnp.exp(scores[chunk] - (largest[:, :1] - bias_of(chunk)))
+            sums[...] += lane_tiles(exponent, jnp.add)
+            acc[...] += dot_nn(exponent.astype(jnp.bfloat16), value_ref[chunk_rows(chunk), :])
+
+        total = jnp.sum(sums[...], axis=1, keepdims=True)
+        inverse = 1.0 / total
+        log_total = largest[...] + jnp.log(total)
+        attended = jnp.zeros((BLOCK, PAD), jnp.float32)
+        for head in range(LOCAL_HEADS):
+            part = slice(head * BLOCK, (head + 1) * BLOCK)
+            attended += acc[part, :] * inverse[part] * head_mask(head, 1.0, jnp.float32)
+            total_ref[slot, head : head + 1, :] = jnp.transpose(log_total[part, :])[:1, :]
+        out_ref[slot] = attended.astype(jnp.bfloat16)
+
+        @pl.when(block != mine)
+        def _():
+            push(
+                out_ref.at[slot],
+                attended_ref.at[z],
+                out_send,
+                out_recv,
+                slot,
+                z,
+                device(slot, lax.rem(core + slot, 2)),
+            ).start()
+
+        @pl.when(block == mine)
+        def _():
+            attended_ref[z] = out_ref[slot]
+
+    for copy in copies:
+        copy.wait_send()
+
+    @pl.loop(0, CHIPS)
+    def _(slot):
+        @pl.when(slot * 2 + lax.rem(core + slot, 2) != mine)
+        def _():
+            push(
+                out_ref.at[slot],
+                attended_ref.at[slot],
+                out_send,
+                out_recv,
+                slot,
+                slot,
+                device(z, 1 - core),
+            ).wait_send()
+
+        @pl.when((slot != z) | (lax.rem(core + z, 2) != core))
+        def _():
+            landed(attended_ref.at[slot], out_send, out_recv, slot)
+
+
+def vmem():
+    return pl.BlockSpec(memory_space=pltpu.VMEM)
+
+
+def smem():
+    return pl.BlockSpec(memory_space=pltpu.SMEM)
+
+
+def front(kind, tokens, gain, weight):
+    half_type = jnp.bfloat16
+    shapes = [
+        jax.ShapeDtypeStruct((8, BLOCK, 768), half_type),
+        jax.ShapeDtypeStruct((8, BLOCK, PAD), half_type),
+        jax.ShapeDtypeStruct((LONG, PAD), half_type),
+        jax.ShapeDtypeStruct((LONG, PAD), half_type),
+        jax.ShapeDtypeStruct((CHIPS, BLOCK, PAD), half_type),
+        jax.ShapeDtypeStruct((CHIPS, 8, BLOCK), jnp.float32),
+        jax.ShapeDtypeStruct((CHIPS, BLOCK, PAD), half_type),
+    ]
+    return pl.pallas_call(
+        front_kernel,
+        out_shape=shapes,
+        in_specs=[smem(), vmem(), vmem(), vmem()],
+        out_specs=[vmem()] * len(shapes),
+        scratch_shapes=[
+            pltpu.VMEM((STACK, PAD), half_type),
+            pltpu.VMEM((CHUNKS, STACK, CHUNK), jnp.float32),
+            pltpu.VMEM((STACK, 128), jnp.float32),
+            pltpu.VMEM((STACK, 128), jnp.float32),
+            pltpu.VMEM((STACK, PAD), jnp.float32),
+            pltpu.SemaphoreType.DMA((8,)),
+            pltpu.SemaphoreType.DMA((8,)),
+            pltpu.SemaphoreType.DMA((CHIPS,)),
+            pltpu.SemaphoreType.DMA((CHIPS,)),
+        ],
+        compiler_params=pltpu.CompilerParams(
+            collective_id=0, has_side_effects=True, vmem_limit_bytes=56 * 2**20
+        ),
+    )(kind, tokens, gain, weight)
+
+
+def back_kernel(
+    kind_ref,
+    grad_ref,
+    query_ref,
+    key_ref,
+    value_ref,
+    out_ref,
+    total_ref,
+    weight_ref,
+    hidden_ref,
+    result_ref,
+    weight_grad_ref,
+    grad_out,
+    stacked,
+    grad_stacked,
+    grad_query,
+    grad_key,
+    grad_value,
+    projected,
+    part_sib,
+    part_own,
+    land_sib,
+    land_half,
+    land_full,
+    grad_send,
+    grad_recv,
+    sib_send,
+    sib_recv,
+    ring_send,
+    ring_recv,
 ):
-    rows_here = queries.shape[0]
-    grad_query, row_delta, probs, grad_scores = query_part(
-        queries, keys_whole, values_whole, seq_kind, start_row, score_scale, log_totals, grad_att
-    )
-    length = keys_whole.shape[0]
-    query_heads = queries.reshape(rows_here, HEADS, HD)
-    grad_heads = grad_att.reshape(rows_here, HEADS, HD)
-    grad_key = (
-        jnp.einsum("hqk,qhd->khd", grad_scores, query_heads, preferred_element_type=jnp.float32)
-        * score_scale
-    )
-    grad_value = jnp.einsum(
-        "hqk,qhd->khd", probs.astype(jnp.bfloat16), grad_heads, preferred_element_type=jnp.float32
-    )
-    return (
-        grad_query,
-        grad_key.reshape(length, HEADS * HD),
-        grad_value.reshape(length, HEADS * HD),
-    )
+    z, core = here()
+    mine = z * 2 + core
+    up, down, far = lax.rem(z + 1, CHIPS), lax.rem(z + 3, CHIPS), lax.rem(z + 2, CHIPS)
+    barrier = pltpu.get_barrier_semaphore()
+    greet(barrier)
+    grad_key[...] = jnp.zeros_like(grad_key)
+    grad_value[...] = jnp.zeros_like(grad_value)
+    projected[...] = jnp.zeros_like(projected)
+    pl.semaphore_wait(barrier, 7)
+    owner_core = lax.rem(core + z, 2)
+
+    @pl.loop(0, CHIPS)
+    def _(step):
+        chip = lax.rem(z + step, CHIPS)
+        mine_too = (chip == z) & (owner_core == core)
+
+        @pl.when(jnp.logical_not(mine_too))
+        def _():
+            push(
+                grad_ref.at[chip],
+                grad_out.at[z],
+                grad_send,
+                grad_recv,
+                chip,
+                z,
+                device(chip, owner_core),
+            ).start()
+
+        @pl.when(mine_too)
+        def _():
+            grad_out[z] = grad_ref[chip]
+
+    kind_bias = kind_ref[0].astype(jnp.float32) * NEGATIVE
+
+    @pl.loop(0, CHIPS)
+    def _(step):
+        slot = lax.rem(z + step, CHIPS)
+        block = slot * 2 + lax.rem(core + slot, 2)
+
+        @pl.when(block != mine)
+        def _():
+            landed(grad_out.at[slot], grad_send, grad_recv, slot)
+
+        queries = query_ref[block]
+        grads = grad_out[slot]
+        products = grads.astype(jnp.float32) * out_ref[slot].astype(jnp.float32)
+        selector = jnp.concatenate(
+            [head_mask(head, 1.0, jnp.float32) for head in range(LOCAL_HEADS)]
+            + [jnp.zeros((8 - LOCAL_HEADS, PAD), jnp.float32)],
+            axis=0,
+        )
+        deltas = lax.dot_general(
+            selector,
+            products,
+            (((1,), (1,)), ((), ())),
+            preferred_element_type=jnp.float32,
+            precision=lax.Precision.HIGHEST,
+        )
+        for head in range(LOCAL_HEADS):
+            part = slice(head * BLOCK, (head + 1) * BLOCK)
+            stacked[part, :] = queries * head_mask(head, HD ** (-0.5), jnp.bfloat16)
+            grad_stacked[part, :] = grads * head_mask(head, 1.0, jnp.bfloat16)
+        totals = total_ref[slot]
+        delta_row = jnp.concatenate(
+            [deltas[head : head + 1, :] for head in range(LOCAL_HEADS)], axis=1
+        )
+        total_row = jnp.concatenate(
+            [totals[head : head + 1, :] for head in range(LOCAL_HEADS)], axis=1
+        )
+
+        def work(chunk, is_last):
+            rows = pl.ds(pl.multiple_of(chunk * CHUNK, CHUNK), CHUNK)
+            keys, values = key_ref[rows, :], value_ref[rows, :]
+            bias = jnp.where((slot >= 2) & (chunk < 2), kind_bias, 0.0)
+            probs = jnp.exp(dot_nt(keys, stacked[...]) - (total_row - bias))
+            if is_last:
+                row = lax.broadcasted_iota(jnp.int32, (CHUNK, STACK), 0)
+                column = lax.broadcasted_iota(jnp.int32, (CHUNK, STACK), 1)
+                allowed = row - lax.rem(column, BLOCK) <= (block - 2 * slot) * BLOCK
+                probs = jnp.where(allowed, probs, 0.0)
+            grad_probs = dot_nt(values, grad_stacked[...])
+            grad_scores = (probs * (grad_probs - delta_row)).astype(jnp.bfloat16)
+            grad_value[rows, :] += dot_nn(probs.astype(jnp.bfloat16), grad_stacked[...])
+            grad_key[rows, :] += dot_nn(grad_scores, stacked[...])
+            return dot_tn(grad_scores, keys)
+
+        grad_query[...] = work(slot, True)
+
+        @pl.loop(0, slot)
+        def _(chunk):
+            grad_query[...] += work(chunk, False)
+
+        combined = jnp.zeros((BLOCK, PAD), jnp.float32)
+        for head in range(LOCAL_HEADS):
+            part = slice(head * BLOCK, (head + 1) * BLOCK)
+            combined += grad_query[part, :] * head_mask(head, HD ** (-0.5), jnp.float32)
+        rows = pl.ds(pl.multiple_of(block * BLOCK, BLOCK), BLOCK)
+        projected[rows, :PAD] = combined.astype(jnp.bfloat16)
+
+    projected[:, PAD : 2 * PAD] = grad_key[...].astype(jnp.bfloat16)
+    projected[:, 2 * PAD :] = grad_value[...].astype(jnp.bfloat16)
+
+    def partial(chip, which):
+        rows = pl.ds(pl.multiple_of((chip * 2 + which) * BLOCK, BLOCK), BLOCK)
+        return dot_nt(projected[rows, :], weight_ref[...])
+
+    def sib_copy(index):
+        return push(
+            part_sib.at[index],
+            land_sib.at[index],
+            sib_send,
+            sib_recv,
+            index,
+            index,
+            device(z, 1 - core),
+        )
+
+    order = (far, up, down, z)
+    for index, chip in enumerate(order):
+        part_sib[index] = partial(chip, 1 - core).astype(jnp.bfloat16)
+        sib_copy(index).start()
+
+    def own(index):
+        value = partial(order[index], core)
+        landed(land_sib.at[index], sib_send, sib_recv, index)
+        return value + land_sib[index].astype(jnp.float32)
+
+    half = BLOCK // 2
+    first, second = pl.ds(0, half), pl.ds(half, half)
+    part_own[0] = own(0).astype(jnp.bfloat16)
+
+    def ring(source, target, index, where):
+        copy = push(source, target, ring_send, ring_recv, index, index, where)
+        copy.start()
+        return copy
+
+    above, below = device(up, core), device(down, core)
+    copies = [
+        ring(part_own.at[0, first], land_half.at[0], 0, above),
+        ring(part_own.at[0, second], land_half.at[1], 1, below),
+    ]
+    part_own[1] = own(1).astype(jnp.bfloat16)
+    copies.append(ring(part_own.at[1, second], land_full.at[0, second], 2, above))
+    part_own[2] = own(2).astype(jnp.bfloat16)
+    copies.append(ring(part_own.at[2, first], land_full.at[1, first], 3, below))
+    result_ref[...] = own(3)
+    landed(land_half.at[0], ring_send, ring_recv, 0)
+    part_own[1, first, :] = (
+        part_own[1, first, :].astype(jnp.float32) + land_half[0].astype(jnp.float32)
+    ).astype(jnp.bfloat16)
+    copies.append(ring(part_own.at[1, first], land_full.at[0, first], 4, above))
+    landed(land_half.at[1], ring_send, ring_recv, 1)
+    part_own[2, second, :] = (
+        part_own[2, second, :].astype(jnp.float32) + land_half[1].astype(jnp.float32)
+    ).astype(jnp.bfloat16)
+    copies.append(ring(part_own.at[2, second], land_full.at[1, second], 5, below))
+
+    for tile in range(3):
+        lanes = slice(tile * PAD, (tile + 1) * PAD)
+        weight_grad_ref[:, lanes] = dot_tn(hidden_ref[...], projected[:, lanes])
+
+    landed(land_full.at[0, second], ring_send, ring_recv, 2)
+    landed(land_full.at[1, first], ring_send, ring_recv, 3)
+    landed(land_full.at[0, first], ring_send, ring_recv, 4)
+    landed(land_full.at[1, second], ring_send, ring_recv, 5)
+    result_ref[...] += land_full[0].astype(jnp.float32) + land_full[1].astype(jnp.float32)
+    for copy in copies:
+        copy.wait_send()
+    for index in range(CHIPS):
+        sib_copy(index).wait_send()
+
+    @pl.loop(0, CHIPS)
+    def _(chip):
+        @pl.when((chip != z) | (owner_core != core))
+        def _():
+            push(
+                grad_ref.at[chip],
+                grad_out.at[chip],
+                grad_send,
+                grad_recv,
+                chip,
+                chip,
+                device(z, 1 - core),
+            ).wait_send()
+
+
+def back(kind, grads, queries, keys, values, out, totals, weight, hidden):
+    half_type = jnp.bfloat16
+    width = 768
+    return pl.pallas_call(
+        back_kernel,
+        out_shape=[
+            jax.ShapeDtypeStruct((BLOCK, width), jnp.float32),
+            jax.ShapeDtypeStruct((width, 3 * PAD), jnp.float32),
+        ],
+        in_specs=[smem()] + [vmem()] * 8,
+        out_specs=[vmem()] * 2,
+        scratch_shapes=[
+            pltpu.VMEM((CHIPS, BLOCK, PAD), half_type),
+            pltpu.VMEM((STACK, PAD), half_type),
+            pltpu.VMEM((STACK, PAD), half_type),
+            pltpu.VMEM((STACK, PAD), jnp.float32),
+            pltpu.VMEM((LONG, PAD), jnp.float32),
+            pltpu.VMEM((LONG, PAD), jnp.float32),
+            pltpu.VMEM((LONG, 3 * PAD), half_type),
+            pltpu.VMEM((CHIPS, BLOCK, width), half_type),
+            pltpu.VMEM((CHIPS, BLOCK, width), half_type),
+            pltpu.VMEM((CHIPS, BLOCK, width), half_type),
+            pltpu.VMEM((2, BLOCK // 2, width), half_type),
+            pltpu.VMEM((2, BLOCK, width), half_type),
+            pltpu.SemaphoreType.DMA((CHIPS,)),
+            pltpu.SemaphoreType.DMA((CHIPS,)),
+            pltpu.SemaphoreType.DMA((CHIPS,)),
+            pltpu.SemaphoreType.DMA((CHIPS,)),
+            pltpu.SemaphoreType.DMA((6,)),
+            pltpu.SemaphoreType.DMA((6,)),
+        ],
+        compiler_params=pltpu.CompilerParams(
+            collective_id=1, has_side_effects=True, vmem_limit_bytes=56 * 2**20
+        ),
+    )(kind, grads, queries, keys, values, out, totals, weight, hidden)
 
 
 def routing(routes, capacity, experts):
@@ -170,24 +630,23 @@
     score_scale = HD ** (-0.5)
     inputs = tokens.astype(jnp.float32)
     normed_one, inverse_one = norm_parts(inputs)
-    hidden_one = (normed_one * norm1_gain).astype(jnp.bfloat16)
-    projected = jnp.einsum(
-        "gtd,de->gte", hidden_one, qkv_weight, preferred_element_type=jnp.float32
-    ).astype(jnp.bfloat16)
-    queries = projected[..., :width]
-    keys_local = projected[..., width : 2 * width]
-    values_local = projected[..., 2 * width :]
-    keys_whole, values_whole = (
-        lax.all_gather(keys_local, "expert", axis=1, tiled=True),
-        lax.all_gather(values_local, "expert", axis=1, tiled=True),
-    )
-
-    def forward_group(group_items):
-        query_rows, key_rows, value_rows, seq_kind = group_items
-        return attend_group(query_rows, key_rows, value_rows, seq_kind, start_row, score_scale)
-
-    attended, log_totals = lax.map(forward_group, (queries, keys_whole, values_whole, group_kind))
-    branch = jnp.einsum("gtd,de->gte", attended, proj_weight, preferred_element_type=jnp.float32)
+    chip = lax.axis_index("expert") // 2
+    chip_columns = lax.dynamic_index_in_dim(
+        qkv_weight.reshape(width, 3, CHIPS, width // CHIPS), chip, axis=2, keepdims=False
+    )
+    chip_weight = jnp.pad(chip_columns, ((0, 0), (0, 0), (0, PAD - width // CHIPS))).reshape(
+        width, 3 * PAD
+    )
+    proj_chips = jnp.pad(
+        proj_weight.reshape(CHIPS, width // CHIPS, width),
+        ((0, 0), (0, PAD - width // CHIPS), (0, 0)),
+    )
+    hidden_all, queries, keys, values, out_heads, totals, attended = front(
+        group_kind, tokens[0], norm1_gain[None], chip_weight
+    )
+    branch = jnp.einsum("ztd,zde->te", attended, proj_chips, preferred_element_type=jnp.float32)[
+        None
+    ]
     residual = inputs + branch
     normed_two, inverse_two = norm_parts(residual)
     hidden_two = (normed_two * norm2_gain).astype(jnp.bfloat16)
@@ -283,57 +742,36 @@
     norm2_gain_grad = jnp.sum(grad_hidden_two * normed_two, axis=(0, 1))
     grad_residual = grad_res + norm_back(grad_hidden_two * norm2_gain, normed_two, inverse_two)
     grad_branch = grad_residual.astype(jnp.bfloat16)
-    proj_grad = jnp.einsum("gtd,gte->de", attended, grad_branch, preferred_element_type=jnp.float32)
+    proj_grad = jnp.einsum(
+        "ztd,te->zde", attended, grad_branch[0], preferred_element_type=jnp.float32
+    )[:, : width // CHIPS].reshape(width, width)
     grad_attended = jnp.einsum(
-        "gte,de->gtd", grad_branch, proj_weight, preferred_element_type=jnp.float32
+        "te,zde->ztd", grad_branch[0], proj_chips, preferred_element_type=jnp.float32
     ).astype(jnp.bfloat16)
-    keys_back, values_back = (keys_whole, values_whole)
-
-    def backward_group(group_items):
-        query_rows, key_rows, value_rows, seq_kind, group_totals, grad_rows = group_items
-        return attend_back(
-            query_rows,
-            key_rows,
-            value_rows,
-            seq_kind,
-            start_row,
-            score_scale,
-            group_totals,
-            grad_rows,
-        )
-
-    grad_queries, grad_keys_whole, grad_values_whole = lax.map(
-        backward_group, (queries, keys_back, values_back, group_kind, log_totals, grad_attended)
-    )
-    grad_keys, grad_values = (
-        lax.psum_scatter(
-            grad_keys_whole.astype(jnp.bfloat16), "expert", scatter_dimension=1, tiled=True
-        ).astype(jnp.float32),
-        lax.psum_scatter(
-            grad_values_whole.astype(jnp.bfloat16), "expert", scatter_dimension=1, tiled=True
-        ).astype(jnp.float32),
-    )
-    grad_projected = jnp.concatenate(
-        [
-            grad_queries.astype(jnp.bfloat16),
-            grad_keys.astype(jnp.bfloat16),
-            grad_values.astype(jnp.bfloat16),
-        ],
-        axis=-1,
-    )
-    qkv_grad = jnp.einsum(
-        "gtd,gte->de", hidden_one, grad_projected, preferred_element_type=jnp.float32
-    )
-    grad_hidden_one = jnp.einsum(
-        "gte,de->gtd", grad_projected, qkv_weight, preferred_element_type=jnp.float32
-    )
+    grad_hidden_one, qkv_grad = back(
+        group_kind,
+        grad_attended,
+        queries,
+        keys,
+        values,
+        out_heads,
+        totals,
+        chip_weight,
+        hidden_all.reshape(LONG, width),
+    )
+    grad_hidden_one = grad_hidden_one[None]
     norm1_gain_grad = jnp.sum(grad_hidden_one * normed_one, axis=(0, 1))
     tokens_grad = grad_residual + norm_back(grad_hidden_one * norm1_gain, normed_one, inverse_one)
     expert_sums = sum_experts(new_in_grad, new_out_grad)
-    everyone = lax.axis_size("dp") * count
-    own = width // everyone
-    matrices = jnp.concatenate([qkv_grad, proj_grad], axis=1).reshape(everyone, own, -1)
-    matrices = lax.psum_scatter(matrices, ("dp", "expert"), scatter_dimension=0, tiled=True)[0]
+    own = width // (lax.axis_size("dp") * count)
+    matrices = jnp.concatenate([qkv_grad, proj_grad], axis=1)
+    matrices = lax.psum_scatter(matrices, "dp", scatter_dimension=0, tiled=True)
+    matrices = lax.all_to_all(
+        matrices.reshape(count, own, -1), "expert", split_axis=0, concat_axis=0, tiled=True
+    )
+    proj_sum = jnp.sum(matrices[..., 3 * PAD :], axis=0)
+    qkv_sum = jnp.sum(matrices[..., : 3 * PAD].reshape(CHIPS, 2, own, 3, PAD), axis=1)
+    qkv_sum = qkv_sum[..., : width // CHIPS].transpose(1, 2, 0, 3).reshape(own, 3 * width)
     narrow = jnp.concatenate(
         [router_grad, norm1_gain_grad[:, None], norm2_gain_grad[:, None]], axis=1
     )
@@ -342,8 +780,8 @@
     narrow = lax.dynamic_slice_in_dim(narrow, first_row, own, axis=0)
     dense_sums = (
         narrow[:, -2],
-        matrices[:, : 3 * width],
-        matrices[:, 3 * width :],
+        qkv_sum,
+        proj_sum,
         narrow[:, -1],
         narrow[:, :-2],
     )

time: 755 us -> 522 us (0.69)
  waiting for transfers between devices: 335 us -> 164 us
  matrix products: 160 us -> 65.3 us
  Pallas kernels: 0 us -> 87.9 us
  other arithmetic: 71.3 us -> 24.4 us
  local copies, waits for them, and re-layouts: 45.4 us -> 19.5 us
  blocking collectives: 107 us -> 132 us
    reduce_scatter x3 -> x1, waiting for transfers between devices: 233 us -> 0.02 us  [on_device(): matrices = lax.psum_scatter(matrices, 'dp', scatter_dimension=0, tiled=True)]
    dot_general x12 -> x3, matrix products: 92 us -> 3.64 us  [the longest x1 1.7 us: on_device(): jnp.einsum('ztd,zde->te', attended, proj_chips, preferred_element_type=jn...]
    pallas_call x0 -> x2, Pallas kernels: none -> 87.9 us  [the longest x1 44.1 us: back(): pl.pallas_call(back_kernel, out_shape=[jax.ShapeDtypeStruct((BLOCK, width...]
    reduce_scatter x1, waiting for transfers between devices: 0.01 us -> 67.7 us  [sum_experts(): lax.psum_scatter(in_grad[None].astype(jnp.bfloat16), 'dp', scatter_dimens...]
    reduce_scatter x1, waiting for transfers between devices: 50.9 us -> 79.2 us  [sum_experts(): lax.psum_scatter(out_grad_weights[None].astype(jnp.bfloat16), 'dp', scatt...]
    all_to_all x0 -> x1, blocking collectives: none -> 20.2 us  [on_device(): lax.all_to_all(grad_received, 'expert', split_axis=2, concat_axis=2, tile...]
    all_gather x2 -> x0, waiting for transfers between devices: 18.5 us -> none  [the longest x1 18.5 us: on_device(): lax.all_gather(keys_local, 'expert', axis=1, tiled=True)]
    convert_element_type x1 -> x0, other arithmetic: 18 us -> none  [query_part(): grad_scores = (probs * (grad_probs - row_delta)).astype(jnp.bfloat16)]
  transfers between devices with their start and end apart: 9 -> 5, of which waited for: 6 -> 3; matrix products, arithmetic and copies ran while one was open for 21% -> 5% of each run, Pallas kernels for 0% -> 0%
where the time goes in v2:
time: 522 us; the launch traced here: 516 us
  waiting for transfers between devices  164 us (31%)
  blocking collectives  132 us (25%)
  Pallas kernels  87.9 us (17%)
  matrix products  65.3 us (13%)
  other arithmetic  24.4 us (5%)
  local copies, waits for them, and re-layouts  19.5 us (4%)
  between operations  15.5 us (3%)
  starting transfers between devices  7.14 us (1%)
    reduce_scatter x1, waiting for transfers between devices, sum_experts(): lax.psum_scatter(out_grad_weights[None].astype(jnp.bfloat16), 'dp', scatt...  79.2 us
    psum x1, blocking collectives, on_device(): narrow = lax.psum(narrow, ('dp', 'expert'))  69 us
    reduce_scatter x1, waiting for transfers between devices, sum_experts(): lax.psum_scatter(in_grad[None].astype(jnp.bfloat16), 'dp', scatter_dimens...  67.7 us
    pallas_call x1, Pallas kernels, back(): pl.pallas_call(back_kernel, out_shape=[jax.ShapeDtypeStruct((BLOCK, width...  44.1 us
    pallas_call x1, Pallas kernels, front(): pl.pallas_call(front_kernel, out_shape=shapes, in_specs=[smem(), vmem(),...  43.9 us
    all_to_all x1, blocking collectives, on_device(): lax.all_to_all(buffers, 'expert', split_axis=2, concat_axis=2, tiled=True)  22.2 us
    all_to_all x1, blocking collectives, on_device(): lax.all_to_all(grad_returned, 'expert', split_axis=2, concat_axis=2, tile...  20.3 us
    all_to_all x1, blocking collectives, on_device(): lax.all_to_all(grad_received, 'expert', split_axis=2, concat_axis=2, tile...  20.2 us
  transfers between devices with their start and end apart: 5, of which 3 were waited for; matrix products, arithmetic and copies ran while one was open for 5% of the time, Pallas kernels for 0%

profile of v2, /device:TPU:0, one launch (start us, length us, event | category | flops | bytes accessed | tf_op | source)
XLA Modules:
  0.0 515.5 jit_solution(5320718625313450948)
XLA Ops:
  10.9 5.7 %copy.53 = bf16[768,2304]{0,1:T(8,128)(2,1)} copy(bf16[768,2304]{1,0:T(8,128)(2,1)} %param.17) | data formatting | bytes 7077888 | tf_op args[4]
  18.1 1.5 copy.54.weight_ref
  19.5 43.9 %shard_map.196 = (bf16[8,256,768]{2,1,0:T(8,128)(2,1)}, bf16[8,256,256]{2,1,0:T(8,128)(2,1)}, bf16[2048,256]{1,0:T(8,128)(2,1)}, bf16[2048,256]{1,0:T(8,128)(2,1...) custom-call(s32[1]{0:T(128)S(6)} %copy.88.kind_ref, ...), custom_call_target="tpu_custom_call" | custom-call | tf_op jit(solution)/shard_map/pallas_call | solution.py:303
  63.4 1.7 fusion.230
  66.7 22.2 %all_to_all.25 = bf16[1,2,8,48,768]{4,3,1,0,2:T(8,128)(2,1)S(1)} all-to-all(bf16[1,2,8,48,768]{4,3,1,0,2:T(8,128)(2,1)S(1)} %copy.58), channel_id=1, replica_groups=mesh['dp'=16,'expert'=8] {'expert'}, dimensions={2} | all-to-all | bytes 2359296 | tf_op jit(solution)/shard_map/all_to_all | solution.py:666
  88.9 6.0 %fusion.139 = (u8[48,3072]{1,0:T(8,128)(4,1)S(1)}, u8[48,3072]{1,0:T(8,128)(4,1)S(1)}, f32[8,48,3072]{2,1,0:T(8,128)S(1)}) fusion(bf16[1,768,3072]{2,1,0:T(8,128)(2,1)} %param.23, bf16[1,2,8,48,768]{4,3,1,0,2:T(8,128)(2,1)S(1)} %all_to_all.25), kind=kOutput, calls=%fused_computation.139 | convolution fusion | flops 1826979840 | bytes 10321920 | tf_op jit(solution)/shard_map/gnsd,df->gnsf/dot_general | solution.py:670
  94.9 10.5 %fusion.5 = bf16[8,48,3072]{2,1,0:T(8,128)(2,1)S(1)} fusion(f32[8,48,3072]{2,1,0:T(8,128)S(1)} %get-tuple-element.90, u8[48,3072]{1,0:T(8,128)(4,1)S(1)} %get-tuple-element.66, u8[48,3072]{1,0:T(8,128)(4,1)S(1)} %get-tuple-element.65), kind=kLoop, calls=%fused_computation.11 | loop fusion | flops 82575360 | bytes 7372800 | tf_op jit(solution)/shard_map/convert_element_type | solution.py:674
  105.4 1.4 copy-done.4
  106.8 2.0 fusion.117
  108.9 3.0 fusion.138
  111.9 13.4 %fusion.123 = bf16[1,1,8,48,768]{4,3,2,1,0:T(8,128)(2,1)S(1)} fusion(bf16[1,3072,768]{2,1,0:T(8,128)(2,1)S(1)} %bitcast.268, f32[8,48,3072]{2,1,0:T(8,128)S(1)} %get-tuple-element.91, u8[48,3072]{1,0:T(8,128)(4,1)S(1)} %get-tuple-element.64, u8[48,3072]{1,0:T(8,128)(4,1)S(1)} %get-tuple-element.63), kind=kOutput, calls=%fused_computation.129 | convolution fusion | flops 1894809600 | bytes 10321920 | tf_op jit(solution)/shard_map/gnsf,fd->gnsd/dot_general | solution.py:675
  126.6 3.6 all-to-all-start.1
  130.5 17.0 %all-to-all-done.1 = bf16[1,2,8,48,768]{4,3,1,0,2:T(8,128)(2,1)S(1)} async-done(((bf16[1,2,8,48,768]{4,3,1,0,2:T(8,128)(2,1)}), bf16[1,2,8,48,768]{4,3,1,0,2:T(8,128)(2,1)S(1)}, u32[]{:S(2)}, u32[]{:S(2)}) %all-to-all-start.1) | async-done | bytes 1179680 | tf_op jit(solution)/shard_map/all_to_all | solution.py:680
  149.3 20.3 %all_to_all.26 = bf16[1,2,8,48,768]{4,3,1,0,2:T(8,128)(2,1)S(1)} all-to-all(bf16[1,2,8,48,768]{4,3,1,0,2:T(8,128)(2,1)S(1)} %copy.63), channel_id=1, replica_groups=mesh['dp'=16,'expert'=8] {'expert'}, dimensions={2} | all-to-all | bytes 2359296 | tf_op jit(solution)/shard_map/all_to_all | solution.py:713
  169.7 5.1 fusion.17
  174.8 1.4 copy-done.16
  176.2 2.0 fusion.120
  178.2 10.1 %fusion.128 = bf16[1,1,8,48,768]{4,3,2,1,0:T(8,128)(2,1)} fusion(bf16[1,768,3072]{2,1,0:T(8,128)(2,1)} %param.21, f32[8,48,3072]{2,1,0:T(8,128)} %copy-done.17, bf16[1,3072,768]{2,1,0:T(8,128)(2,1)} %param.22, bf16[1,2,8,48,768]{4,3,1,0,2:T(8,128)(2,1)S(1)} %all_to_all.26), kind=kOutput, calls=%fused_computation.130 | convolution fusion | flops 3635970048 | bytes 15335424 | tf_op jit(solution)/shard_map/gnsf,df->gnsd/dot_general | solution.py:728
  189.6 20.2 %all_to_all.27 = bf16[1,2,8,48,768]{4,3,1,0,2:T(8,128)(2,1)S(1)} all-to-all(bf16[1,2,8,48,768]{4,3,1,0,2:T(8,128)(2,1)S(1)} %copy.66), channel_id=1, replica_groups=mesh['dp'=16,'expert'=8] {'expert'}, dimensions={2} | all-to-all | bytes 2359296 | tf_op jit(solution)/shard_map/all_to_all | solution.py:735
  211.6 1.4 fusion.133.grad_ref
  213.6 44.1 %shard_map.197 = (f32[256,768]{1,0:T(8,128)}, f32[768,768]{1,0:T(8,128)}) custom-call(s32[1]{0:T(128)S(6)} %copy.88.kind_ref, bf16[4,256,256]{2,1,0:T(8,128)(2,1)} %fusion.133.grad_ref, bf16[8,256,256]{2,1,0:T(8,128)(2,1)} %get-tuple-element.19.query_ref, bf16[2048,256]{1,0:T(8,128)(2,1)} %get-tuple-element.20.key_ref, ...), custom_call_target="tpu_custom_call" | custom-call | tf_op jit(solution)/shard_map/pallas_call | solution.py:545
  257.7 4.6 pad_maximum_fusion
  262.3 6.6 %fusion.46 = bf16[1,768,3072]{2,1,0:T(8,128)(2,1)} fusion(bf16[8,48,3072]{2,1,0:T(8,128)(2,1)} %copy-done.16, bf16[1,2,8,48,768]{4,3,1,0,2:T(8,128)(2,1)} %copy-done.8), kind=kOutput, calls=%fused_computation.76 | convolution fusion | flops 1814298624 | bytes 7667712 | tf_op jit(solution)/shard_map/gnsd,gnsf->df/dot_general | solution.py:725
  269.1 6.6 %fusion.47 = bf16[1,3072,768]{2,1,0:T(8,128)(2,1)} fusion(bf16[8,48,3072]{2,1,0:T(8,128)(2,1)} %copy-done.4, bf16[1,2,8,48,768]{4,3,1,0,2:T(8,128)(2,1)} %copy-done.9), kind=kOutput, calls=%fused_computation.77 | convolution fusion | flops 1814298624 | bytes 7667712 | tf_op jit(solution)/shard_map/gnsf,gnsd->fd/dot_general | solution.py:722
  276.3 2.8 fusion.116
  279.5 69.0 %psum.7 = f32[768,18]{0,1:T(8,128)S(1)} all-reduce(f32[768,18]{0,1:T(8,128)S(1)} %pad_maximum_fusion.3), channel_id=1, replica_groups=mesh['dp'=16,'expert'=8] {'dp','expert'}, use_global_device_ids=true, to_apply=%region_18.19 | all-reduce | flops 13824 | bytes 110592 | tf_op jit(solution)/shard_map/psum | solution.py:778
  350.0 1.8 reshape.1331
  351.8 3.5 all-to-all-start.4
  356.4 67.7 %reduce-scatter.6.cloned.1.call-done = bf16[1,48,3072]{2,1,0:T(8,128)(2,1)} async-done(((bf16[1,768,3072]{2,1,0:T(8,128)(2,1)}), bf16[1,48,3072]{2,1,0:T(8,128)(2,1)}) %reduce-scatter.6.cloned.1.call-update) | async-done | bytes 294928 | tf_op jit(solution)/shard_map/reduce_scatter | solution.py:601
  424.1 1.8 convert_element_type.348
  425.9 79.2 %reduce-scatter.8.cloned.1.call-done = bf16[1,192,768]{2,1,0:T(8,128)(2,1)} async-done(((bf16[1,3072,768]{2,1,0:T(8,128)(2,1)}), bf16[1,192,768]{2,1,0:T(8,128)(2,1)}) %reduce-scatter.8.cloned.1.call-update) | async-done | bytes 294928 | tf_op jit(solution)/shard_map/reduce_scatter | solution.py:604
  505.1 1.8 convert_element_type.351
  (130 shorter events, 18.2 us)
Async XLA Ops:
  7.2 123.1 %copy-start = (bf16[768,16]{0,1:T(8,128)(2,1)S(1)}, bf16[768,16]{0,1:T(8,128)(2,1)}, u32[]{:S(2)}) copy-start(bf16[768,16]{0,1:T(8,128)(2,1)} %param.20) | copy-start | bytes 73732
  16.6 46.8 %copy-start.1 = (bf16[1,256,768]{2,1,0:T(8,128)(2,1)S(1)}, bf16[1,256,768]{2,1,0:T(8,128)(2,1)}, u32[]{:S(2)}) copy-start(bf16[1,256,768]{2,1,0:T(8,128)(2,1)} %param.13) | copy-start | bytes 1179652
  16.6 46.8 %copy-start.5 = (bf16[768,768]{1,0:T(8,128)(2,1)S(1)}, bf16[768,768]{1,0:T(8,128)(2,1)}, u32[]{:S(2)}) copy-start(bf16[768,768]{1,0:T(8,128)(2,1)} %param.18) | copy-start | bytes 3538948
  18.0 47.6 %copy-start.15 = (s32[1,256,2]{1,2,0:T(2,128)S(1)}, s32[1,256,2]{1,2,0:T(2,128)}, u32[]{:S(2)}) copy-start(s32[1,256,2]{1,2,0:T(2,128)} %param.15) | copy-start | bytes 6148
  18.0 47.6 %copy-start.13 = (f32[768]{0:T(1024)S(1)}, f32[768]{0:T(1024)}, u32[]{:S(2)}) copy-start(f32[768]{0:T(1024)} %param.19) | copy-start | bytes 9220
  66.7 40.1 %slice-start.2 = ((s8[4718592]{0:T(1024)(128)(4,1)}), s8[4194304]{0:T(1024)(128)(4,1)S(1)}, s32[]{:S(2)}) async-start(s8[4718592]{0:T(1024)(128)(4,1)} %bitcast.263), calls=%async_computation.13 | async-start | bytes 8388608
  88.9 20.0 %copy-start.8 = (bf16[1,2,8,48,768]{4,3,1,0,2:T(8,128)(2,1)}, bf16[1,2,8,48,768]{4,3,1,0,2:T(8,128)(2,1)S(1)}, u32[]{:S(2)}) copy-start(bf16[1,2,8,48,768]{4,3,1,0,2:T(8,128)(2,1)S(1)} %all_to_all.25) | copy-start | bytes 3538948
  88.9 17.9 %slice-start.3 = ((s8[4718592]{0:T(1024)(128)(4,1)}), s8[524288]{0:T(1024)(128)(4,1)S(1)}, s32[]{:S(2)}) async-start(s8[4718592]{0:T(1024)(128)(4,1)} %bitcast.263), calls=%async_computation.14 | async-start | bytes 1048576
  94.8 14.0 %copy-start.3 = (f32[8,48,3072]{2,1,0:T(8,128)}, f32[8,48,3072]{2,1,0:T(8,128)S(1)}, u32[]{:S(2)}) copy-start(f32[8,48,3072]{2,1,0:T(8,128)S(1)} %get-tuple-element.90) | copy-start | bytes 14155780
  94.8 14.0 %slice-start.8 = ((s8[4718592]{0:T(1024)(128)(4,1)}), s8[4194304]{0:T(1024)(128)(4,1)S(1)}, s32[]{:S(2)}) async-start(s8[4718592]{0:T(1024)(128)(4,1)} %bitcast.269), calls=%async_computation.19 | async-start | bytes 8388608
  105.4 1.4 copy-start.4
  106.8 2.1 slice-start.9
  106.8 5.1 slice-start.6
  108.9 3.1 slice-start.7
  111.9 13.5 %copy-start.17 = (f32[8,48,3072]{2,1,0:T(8,128)}, f32[8,48,3072]{2,1,0:T(8,128)S(1)}, u32[]{:S(2)}) copy-start(f32[8,48,3072]{2,1,0:T(8,128)S(1)} %get-tuple-element.91) | copy-start | bytes 14155780
  125.4 22.2 %copy-start.11 = (bf16[1,256,768]{2,1,0:T(8,128)(2,1)S(1)}, bf16[1,256,768]{2,1,0:T(8,128)(2,1)}, u32[]{:S(2)}) copy-start(bf16[1,256,768]{2,1,0:T(8,128)(2,1)} %param.25) | copy-start | bytes 1179652
  126.6 20.9 %all-to-all-start.1 = ((bf16[1,2,8,48,768]{4,3,1,0,2:T(8,128)(2,1)}), bf16[1,2,8,48,768]{4,3,1,0,2:T(8,128)(2,1)S(1)}, u32[]{:S(2)}, u32[]{:S(2)}) async-start(bf16[1,2,8,48,768]{4,3,1,0,2:T(8,128)(2,1)} %copy.61), calls=%async_computation.1 | async-start | bytes 2359296 | tf_op jit(solution)/shard_map/all_to_all | solution.py:680
  130.2 219.8 %reduce-scatter.4.cloned.1.call-start = ((), (), s32[]{:S(2)}) async-start(), calls=%async_computation.8 | async-start | bytes 5013504 | tf_op jit(solution)/shard_map/reduce_scatter | solution.py:768
  147.6 1.6 copy-start.7
  147.6 22.1 %slice-start = ((s8[4718592]{0:T(1024)(128)(4,1)}), s8[4194304]{0:T(1024)(128)(4,1)S(1)}, s32[]{:S(2)}) async-start(s8[4718592]{0:T(1024)(128)(4,1)} %bitcast.226), calls=%async_computation.11 | async-start | bytes 8388608
  148.3 21.4 %slice-start.1 = ((s8[4718592]{0:T(1024)(128)(4,1)}), s8[524288]{0:T(1024)(128)(4,1)S(1)}, s32[]{:S(2)}) async-start(s8[4718592]{0:T(1024)(128)(4,1)} %bitcast.226), calls=%async_computation.12 | async-start | bytes 1048576
  149.2 27.0 %slice-start.4 = ((s8[4718592]{0:T(1024)(128)(4,1)}), s8[4194304]{0:T(1024)(128)(4,1)S(1)}, s32[]{:S(2)}) async-start(s8[4718592]{0:T(1024)(128)(4,1)} %bitcast.265), calls=%async_computation.15 | async-start | bytes 8388608
  169.7 8.6 %copy-start.9 = (bf16[1,2,8,48,768]{4,3,1,0,2:T(8,128)(2,1)}, bf16[1,2,8,48,768]{4,3,1,0,2:T(8,128)(2,1)S(1)}, u32[]{:S(2)}) copy-start(bf16[1,2,8,48,768]{4,3,1,0,2:T(8,128)(2,1)S(1)} %all_to_all.26) | copy-start | bytes 3538948
  169.7 6.5 %slice-start.5 = ((s8[4718592]{0:T(1024)(128)(4,1)}), s8[524288]{0:T(1024)(128)(4,1)S(1)}, s32[]{:S(2)}) async-start(s8[4718592]{0:T(1024)(128)(4,1)} %bitcast.265), calls=%async_computation.16 | async-start | bytes 1048576
  189.6 21.7 %copy-start.12 = (bf16[1,256,768]{2,1,0:T(8,128)(2,1)S(1)}, bf16[1,256,768]{2,1,0:T(8,128)(2,1)}, u32[]{:S(2)}) copy-start(bf16[1,256,768]{2,1,0:T(8,128)(2,1)} %param.25) | copy-start | bytes 1179652
  209.9 1.7 copy-start.6
  210.6 2.4 copy-start.10
  262.3 161.8 %reduce-scatter.6.cloned.1.call-start = ((), (), s32[]{:S(2)}) async-start(), calls=%async_computation.9 | async-start | bytes 5013504 | tf_op jit(solution)/shard_map/reduce_scatter | solution.py:601
  269.0 236.1 %reduce-scatter.8.cloned.1.call-start = ((), (), s32[]{:S(2)}) async-start(), calls=%async_computation.10 | async-start | bytes 5013504 | tf_op jit(solution)/shard_map/reduce_scatter | solution.py:604
  275.7 3.4 copy-start.2
  275.7 3.4 copy-start.14
  351.8 155.1 %all-to-all-start.4 = ((f32[8,6,1536]{2,1,0:T(8,128)}), f32[8,6,1536]{2,1,0:T(8,128)S(1)}, u32[]{:S(2)}, u32[]{:S(2)}) async-start(f32[8,6,1536]{2,1,0:T(8,128)} %reshape.1331), calls=%async_computation.5 | async-start | bytes 786432 | tf_op jit(solution)/shard_map/all_to_all | solution.py:769
  (1 other events, 1.4 us)
Sparse Core Ops, SparseCore 0:
  262.4 80.4 reduce-scatter.3
  346.3 77.7 reduce-scatter.5
  427.5 77.5 reduce-scatter.7
